TPU v7x, 256 devices: a whole 4x4x8 slice. The times are simulated.
256 devices in a mesh: expert: 64 (over x, z, core), dp: 4 (over y).
Axes of the slice: x: 4, y: 4, z: 8, core: 2. Of those that a mesh axis runs over, the one named last changes fastest.
Arguments:
- tokens: bfloat16 [8192, 4096], P('expert'), may hold values from -6 to 6
- cotangent: bfloat16 [8192, 4096], P('expert'), may hold values from -6 to 6
- gates: float32 [8192, 2], P('expert'), may hold values from 0.2 to 1
- routing: int32 [8192, 2], P('expert'), may hold values from 0 to 31, all different within a row; in each aligned block of 128 rows (0 to 127, 128 to 255, ...) at most 16 rows name the same one
- gate_weight: bfloat16 [64, 768, 4096], P('expert', 'dp'), may hold values from -0.09375 to 0.09375
- up_weight: bfloat16 [64, 768, 4096], P('expert', 'dp'), may hold values from -0.09375 to 0.09375
- down_weight: bfloat16 [64, 768, 4096], P('expert', 'dp'), may hold values from -0.15625 to 0.15625
Outputs:
- input_grad: bfloat16 [8192, 4096], P('expert', 'dp')
- gate_grad: bfloat16 [64, 768, 4096], P('expert', 'dp')
- up_grad: bfloat16 [64, 768, 4096], P('expert', 'dp')
- down_grad: bfloat16 [64, 768, 4096], P('expert', 'dp')
Inputs may be any that keep to these rules, and one draw needn't show every extreme that they name: `routing`: each row names 2 different experts. Among the 128 rows of one token group (aligned blocks) no expert is named by more than 16 rows, a bound that some block reaches.
All inputs are finite; a program needn't handle non-finite values.
Results may differ from a plain program's by a relative error of at most 0.012.
Values may be sent and summed in bfloat16 or wider, within the bound.
No kernel may reach another device: no remote copies, remote signals or barrier semaphores. Data moves between devices by JAX's collectives and lax.ppermute only.
A program may use at most 128 MiB of HBM per device.

v0:
```python
import jax
import jax.numpy as jnp
from jax import lax
from jax.sharding import PartitionSpec as P


def owner_work(rows_x, rows_g, w_gate, w_up, w_down):
    contract_rows = (((0,), (0,)), ((), ()))
    contract_cols = (((1,), (1,)), ((), ()))
    gate = lax.dot_general(rows_x, w_gate, contract_cols, preferred_element_type=jnp.float32)
    upval = lax.dot_general(rows_x, w_up, contract_cols, preferred_element_type=jnp.float32)
    sigma = jax.nn.sigmoid(gate)
    active = gate * sigma
    hidden = (active * upval).astype(jnp.bfloat16)
    dhid = lax.dot_general(rows_g, w_down, contract_cols, preferred_element_type=jnp.float32)
    dgate = (dhid * upval * sigma * (1.0 + gate * (1.0 - sigma))).astype(jnp.bfloat16)
    dup = (dhid * active).astype(jnp.bfloat16)
    grad_down = lax.dot_general(
        hidden, rows_g, contract_rows, preferred_element_type=jnp.float32
    ).astype(jnp.bfloat16)
    grad_gate = lax.dot_general(
        dgate, rows_x, contract_rows, preferred_element_type=jnp.float32
    ).astype(jnp.bfloat16)
    grad_up = lax.dot_general(
        dup, rows_x, contract_rows, preferred_element_type=jnp.float32
    ).astype(jnp.bfloat16)
    terms = jnp.dot(dgate, w_gate, preferred_element_type=jnp.float32)
    terms = terms + jnp.dot(dup, w_up, preferred_element_type=jnp.float32)
    return (terms.astype(jnp.bfloat16), grad_gate, grad_up, grad_down)


def per_device(tokens, cotangent, gates, routing, gate_weight, up_weight, down_weight):
    tok_rows, width = tokens.shape
    choose = routing.shape[1]
    experts = lax.axis_size("expert") // 2
    capacity = 2 * tok_rows * choose // experts
    flat_routes = routing.reshape(-1)
    onehot = (flat_routes[:, None] == jnp.arange(experts, dtype=jnp.int32)[None, :]).astype(
        jnp.int32
    )
    ranks = jnp.sum((jnp.cumsum(onehot, axis=0) - 1) * onehot, axis=1)
    places = flat_routes * capacity + ranks
    route_ids = jnp.arange(flat_routes.shape[0], dtype=jnp.int32)
    filler = jnp.zeros((experts * capacity,), jnp.int32).at[places].set(route_ids + 1)
    live = filler > 0
    route = jnp.maximum(filler - 1, 0)
    source_tok = route // choose
    slot_x = jnp.where(live[:, None], tokens[source_tok], jnp.zeros((), tokens.dtype))
    scaled_full = gates.reshape(-1)[route][:, None] * cotangent[source_tok].astype(jnp.float32)
    slot_g = jnp.where(live[:, None], scaled_full, jnp.zeros((), jnp.float32)).astype(jnp.bfloat16)
    w_gate = gate_weight[0]
    w_up = up_weight[0]
    w_down = down_weight[0]
    send_x = jnp.repeat(slot_x.reshape(experts, capacity, width), 2, axis=0)
    send_g = jnp.repeat(slot_g.reshape(experts, capacity, width), 2, axis=0)
    recv_x, recv_g = (
        lax.all_to_all(send_x, "expert", split_axis=0, concat_axis=0, tiled=True),
        lax.all_to_all(send_g, "expert", split_axis=0, concat_axis=0, tiled=True),
    )
    terms, grad_gate, grad_up, grad_down = owner_work(
        recv_x.reshape(-1, width), recv_g.reshape(-1, width), w_gate, w_up, w_down
    )
    back = lax.all_to_all(
        terms.reshape(2 * experts, capacity, width),
        "expert",
        split_axis=0,
        concat_axis=0,
        tiled=True,
    )
    combined = jnp.sum(back.reshape(experts, 2, capacity, width).astype(jnp.float32), axis=1)
    combined = combined.reshape(experts * capacity, -1)
    per_route = combined[places].reshape(tok_rows, choose, -1)
    token_sums = jnp.sum(per_route, axis=1)
    input_grad = lax.psum_scatter(token_sums, "dp", scatter_dimension=1, tiled=True).astype(
        jnp.bfloat16
    )
    return (input_grad, grad_gate[None], grad_up[None], grad_down[None])


def solution(mesh):
    placed = (
        P("expert", None),
        P("expert", None),
        P("expert", None),
        P("expert", None),
        P("expert", "dp", None),
        P("expert", "dp", None),
        P("expert", "dp", None),
    )
    return jax.shard_map(
        per_device,
        mesh=mesh,
        in_specs=placed,
        out_specs=(
            P("expert", "dp"),
            P("expert", "dp", None),
            P("expert", "dp", None),
            P("expert", "dp", None),
        ),
        check_vma=False,
    )
```

profile of v0, /device:TPU:30, one launch (start us, length us, event | category | flops | bytes accessed | tf_op | source)
XLA Modules:
  0.0 713.6 jit_solution(3511484324756139112)
XLA Ops:
  7.2 0.0 copy-start
  7.2 0.8 broadcast_multiply_fusion
  8.0 0.8 copy.12
  8.8 0.1 eq.29
  8.9 0.1 eq.25
  9.1 0.1 copy.11
  9.2 0.1 mul.53
  9.3 0.6 reduce-window.6
  9.9 0.2 slice_reduce_fusion
  10.2 0.1 fusion.17
  10.3 1.4 scatter_custom_fusion
  11.7 0.1 broadcast_in_dim.52
  11.8 9.9 %gather_fusion.2 = bf16[512,4096]{1,0:T(8,128)(2,1)} fusion(bf16[128,4096]{1,0:T(8,128)(2,1)} %param.7, s32[1024]{0:T(1024)S(1)} %get-tuple-element.8), kind=kCustom, calls=%fused_computation.2 | custom fusion | bytes 8390656 | tf_op jit(solution)/shard_map/gather | solution.py:48
  21.7 2.5 broadcast_select_fusion
  24.3 4.3 broadcast_in_dim.59
  28.5 13.0 %all-to-all-start.1 = ((bf16[64,16,4096]{2,1,0:T(8,128)(2,1)}), bf16[64,16,4096]{2,1,0:T(8,128)(2,1)}, u32[]{:S(2)}, u32[]{:S(2)}) async-start(bf16[64,16,4096]{2,1,0:T(8,128)(2,1)} %bitcast.63), calls=%async_computation.1 | async-start | bytes 16777216 | tf_op jit(solution)/shard_map/all_to_all | solution.py:57
  41.5 0.0 copy-done.6
  41.5 0.0 copy-start.2
  41.5 0.1 copy.15
  41.6 0.1 reshape.106
  41.8 3.5 gather_fusion
  45.3 0.1 mul.55
  45.4 4.4 gather_fusion.1
  49.8 6.3 fusion.1
  56.1 168.5 %all-to-all-done.1 = bf16[64,16,4096]{2,1,0:T(8,128)(2,1)} async-done(((bf16[64,16,4096]{2,1,0:T(8,128)(2,1)}), bf16[64,16,4096]{2,1,0:T(8,128)(2,1)}, u32[]{:S(2)}, u32[]{:S(2)}) %all-to-all-start.1) | async-done | bytes 8388640 | tf_op jit(solution)/shard_map/all_to_all | solution.py:57
  224.6 6.5 broadcast_in_dim.57
  231.1 9.3 %all-to-all-start = ((bf16[64,16,4096]{2,1,0:T(8,128)(2,1)}), bf16[64,16,4096]{2,1,0:T(8,128)(2,1)}, u32[]{:S(2)}, u32[]{:S(2)}) async-start(bf16[64,16,4096]{2,1,0:T(8,128)(2,1)} %bitcast.64), calls=%async_computation | async-start | bytes 16777216 | tf_op jit(solution)/shard_map/all_to_all | solution.py:58
  240.4 0.0 copy-start.3
  240.4 7.3 %fusion.7 = f32[1024,192]{0,1:T(8,128)} fusion(bf16[1024,4096]{1,0:T(8,128)(2,1)} %bitcast.9, bf16[1,192,4096]{2,1,0:T(8,128)(2,1)S(1)} %copy-done), kind=kOutput, calls=%fused_computation.19 | convolution fusion | flops 1610612736 | bytes 10747904 | tf_op jit(solution)/shard_map/dot_general | solution.py:10
  247.7 7.2 %fusion.10 = f32[1024,192]{0,1:T(8,128)} fusion(bf16[1024,4096]{1,0:T(8,128)(2,1)} %bitcast.9, bf16[1,192,4096]{2,1,0:T(8,128)(2,1)S(1)} %copy-done.3), kind=kOutput, calls=%fused_computation.22 | convolution fusion | flops 1610612736 | bytes 10747904 | tf_op jit(solution)/shard_map/dot_general | solution.py:11
  254.9 168.6 %all-to-all-done = bf16[64,16,4096]{2,1,0:T(8,128)(2,1)} async-done(((bf16[64,16,4096]{2,1,0:T(8,128)(2,1)}), bf16[64,16,4096]{2,1,0:T(8,128)(2,1)}, u32[]{:S(2)}, u32[]{:S(2)}) %all-to-all-start) | async-done | bytes 8388640 | tf_op jit(solution)/shard_map/all_to_all | solution.py:58
  423.5 7.3 %multiply_convert_fusion.1 = (bf16[1024,192]{0,1:T(8,128)(2,1)S(1)}, bf16[1024,192]{0,1:T(8,128)(2,1)S(1)}) fusion(f32[1024,192]{0,1:T(8,128)} %fusion.7, f32[1024,192]{0,1:T(8,128)} %fusion.10, bf16[1024,4096]{1,0:T(8,128)(2,1)} %bitcast.5, bf16[1,192,4096]{2,1,0:T(8,128)(2,1)} %param.13), kind=kOutput, calls=%fused_computation.27 | convolution fusion | flops 1613168640 | bytes 12320768 | tf_op jit(solution)/shard_map/dot_general | solution.py:15
  430.8 0.0 copy-start.4
  430.8 8.1 %fusion.5 = f32[1024,4096]{1,0:T(8,128)} fusion(bf16[1024,192]{0,1:T(8,128)(2,1)S(1)} %get-tuple-element.5, bf16[1,192,4096]{2,1,0:T(8,128)(2,1)S(1)} %copy-done), kind=kOutput, calls=%fused_computation.17 | convolution fusion | flops 1610612736 | bytes 18743296 | tf_op jit(solution)/shard_map/dot_general | solution.py:27
  438.9 11.3 %add_convert_fusion = bf16[1024,4096]{1,0:T(8,128)(2,1)} fusion(f32[1024,4096]{1,0:T(8,128)} %fusion.5, bf16[1024,192]{0,1:T(8,128)(2,1)S(1)} %get-tuple-element.4, bf16[1,192,4096]{2,1,0:T(8,128)(2,1)S(1)} %copy-done.3), kind=kOutput, calls=%fused_computation.6 | convolution fusion | flops 1619001344 | bytes 27131904 | tf_op jit(solution)/shard_map/dot_general | solution.py:28
  450.2 8.6 %all-to-all-start.2 = ((bf16[64,16,4096]{2,1,0:T(8,128)(2,1)}), bf16[64,16,4096]{2,1,0:T(8,128)(2,1)}, u32[]{:S(2)}, u32[]{:S(2)}) async-start(bf16[64,16,4096]{2,1,0:T(8,128)(2,1)} %bitcast.62), calls=%async_computation.2 | async-start | bytes 16777216 | tf_op jit(solution)/shard_map/all_to_all | solution.py:63
  458.8 0.0 reduce-scatter.2.cloned.1.call-start
  458.9 183.3 %all-to-all-done.2 = bf16[64,16,4096]{2,1,0:T(8,128)(2,1)} async-done(((bf16[64,16,4096]{2,1,0:T(8,128)(2,1)}), bf16[64,16,4096]{2,1,0:T(8,128)(2,1)}, u32[]{:S(2)}, u32[]{:S(2)}) %all-to-all-start.2) | async-done | bytes 8388640 | tf_op jit(solution)/shard_map/all_to_all | solution.py:63
  642.1 9.4 %convert_reduce_fusion = f32[32,16,4096]{2,1,0:T(8,128)} fusion(bf16[64,16,4096]{2,1,0:T(8,128)(2,1)} %all-to-all-done.2), kind=kLoop, calls=%fused_computation.5 | loop fusion | flops 6291456 | bytes 16777216 | tf_op jit(solution)/shard_map/reduce_sum | solution.py:70
  651.6 9.0 %gather_fusion.3 = f32[256,4096]{1,0:T(8,128)} fusion(f32[512,4096]{1,0:T(8,128)} %bitcast.61, s32[1024]{0:T(1024)S(1)} %pad_clamp_fusion), kind=kCustom, calls=%fused_computation.3 | custom fusion | bytes 8389632 | tf_op jit(solution)/shard_map/gather | solution.py:72
  660.6 6.0 reshape.113
  666.6 8.8 %reduce_sum.32 = f32[128,4096]{1,0:T(8,128)} reduce(f32[128,2,4096]{2,1,0:T(2,128)} %reshape.113, f32[]{:T(128)} %constant.39.clone.1), dimensions={1}, to_apply=%region_5.6 | reduce | flops 524288 | bytes 6291460 | tf_op jit(solution)/shard_map/reduce_sum | solution.py:73
  675.4 0.0 reduce-scatter.2.cloned.1.call-update
  675.5 6.3 fusion.3
  681.8 6.4 fusion.2
  688.2 6.6 fusion.4
  694.8 9.9 %reduce-scatter.2.cloned.1.call-done = f32[128,1024]{1,0:T(8,128)} async-done(((f32[128,4096]{1,0:T(8,128)}), f32[128,1024]{1,0:T(8,128)}) %reduce-scatter.2.cloned.1.call-update) | async-done | bytes 524304 | tf_op jit(solution)/shard_map/reduce_scatter | solution.py:74
  704.7 1.8 convert_element_type.55
  (22 shorter events, 0.1 us)
Async XLA Ops:
  7.2 233.2 %copy-start = (bf16[1,192,4096]{2,1,0:T(8,128)(2,1)S(1)}, bf16[1,192,4096]{2,1,0:T(8,128)(2,1)}, u32[]{:S(2)}) copy-start(bf16[1,192,4096]{2,1,0:T(8,128)(2,1)} %param.11) | copy-start | bytes 4718596
  28.5 13.0 %copy-start.6 = (f32[128,2]{0,1:T(2,128)S(1)}, f32[128,2]{0,1:T(2,128)}, u32[]{:S(2)}) copy-start(f32[128,2]{0,1:T(2,128)} %param.9) | copy-start | bytes 3076
  28.5 196.1 %all-to-all-start.1 = ((bf16[64,16,4096]{2,1,0:T(8,128)(2,1)}), bf16[64,16,4096]{2,1,0:T(8,128)(2,1)}, u32[]{:S(2)}, u32[]{:S(2)}) async-start(bf16[64,16,4096]{2,1,0:T(8,128)(2,1)} %bitcast.63), calls=%async_computation.1 | async-start | bytes 16777216 | tf_op jit(solution)/shard_map/all_to_all | solution.py:57
  41.5 3.9 copy-start.2
  231.1 192.4 %all-to-all-start = ((bf16[64,16,4096]{2,1,0:T(8,128)(2,1)}), bf16[64,16,4096]{2,1,0:T(8,128)(2,1)}, u32[]{:S(2)}, u32[]{:S(2)}) async-start(bf16[64,16,4096]{2,1,0:T(8,128)(2,1)} %bitcast.64), calls=%async_computation | async-start | bytes 16777216 | tf_op jit(solution)/shard_map/all_to_all | solution.py:58
  240.4 7.3 %copy-start.3 = (bf16[1,192,4096]{2,1,0:T(8,128)(2,1)S(1)}, bf16[1,192,4096]{2,1,0:T(8,128)(2,1)}, u32[]{:S(2)}) copy-start(bf16[1,192,4096]{2,1,0:T(8,128)(2,1)} %param.12) | copy-start | bytes 4718596
  430.8 8.1 %copy-start.4 = (bf16[1024,192]{0,1:T(8,128)(2,1)}, bf16[1024,192]{0,1:T(8,128)(2,1)S(1)}, u32[]{:S(2)}) copy-start(bf16[1024,192]{0,1:T(8,128)(2,1)S(1)} %get-tuple-element.4) | copy-start | bytes 1179652
  450.2 191.9 %all-to-all-start.2 = ((bf16[64,16,4096]{2,1,0:T(8,128)(2,1)}), bf16[64,16,4096]{2,1,0:T(8,128)(2,1)}, u32[]{:S(2)}, u32[]{:S(2)}) async-start(bf16[64,16,4096]{2,1,0:T(8,128)(2,1)} %bitcast.62), calls=%async_computation.2 | async-start | bytes 16777216 | tf_op jit(solution)/shard_map/all_to_all | solution.py:63
  458.8 245.9 %reduce-scatter.2.cloned.1.call-start = ((), (), s32[]{:S(2)}) async-start(), calls=%async_computation.4 | async-start | bytes 2621440 | tf_op jit(solution)/shard_map/reduce_scatter | solution.py:74
  666.6 8.9 %copy-start.5 = (bf16[1024,192]{0,1:T(8,128)(2,1)S(1)}, bf16[1024,192]{0,1:T(8,128)(2,1)}, u32[]{:S(2)}) copy-start(bf16[1024,192]{0,1:T(8,128)(2,1)} %copy-done.4) | copy-start | bytes 1179652
  681.8 6.5 copy-start.7
  681.8 6.5 copy-start.8
  688.2 18.3 %copy-start.1 = (bf16[1,192,4096]{2,1,0:T(8,128)(2,1)S(1)}, bf16[1,192,4096]{2,1,0:T(8,128)(2,1)}, u32[]{:S(2)}) copy-start(bf16[1,192,4096]{2,1,0:T(8,128)(2,1)} %param.11) | copy-start | bytes 4718596
Sparse Core Ops, SparseCore 0:
  675.6 29.1 reduce-scatter.1
where the time goes:
time: 723 us; the launch traced here: 714 us
  waiting for transfers between devices  530 us (73%)
  matrix products  60.5 us (8%)
  local copies, waits for them, and re-layouts  46.9 us (6%)
  starting transfers between devices  30.8 us (4%)
  other arithmetic  30.5 us (4%)
  between operations  14.4 us (2%)
    all_to_all x1, waiting for transfers between devices, per_device(): lax.all_to_all(terms.reshape(2 * experts, capacity, width), 'expert', spl...  183 us
    all_to_all x1, waiting for transfers between devices, per_device(): lax.all_to_all(send_g, 'expert', split_axis=0, concat_axis=0, tiled=True)  169 us
    all_to_all x1, waiting for transfers between devices, per_device(): lax.all_to_all(send_x, 'expert', split_axis=0, concat_axis=0, tiled=True)  169 us
  transfers between devices with their start and end apart: 4, of which 4 were waited for; matrix products, arithmetic and copies ran while one was open for 7% of the time, Pallas kernels for 0%

commit v1 on v0

v1 whole, which is shorter than its diff:
```python
import functools

import jax
import jax.numpy as jnp
from jax import lax
from jax.experimental import pallas as pl
from jax.experimental.pallas import tpu as pltpu
from jax.sharding import PartitionSpec as P

F32 = jnp.float32
BF16 = jnp.bfloat16
NT = (((1,), (1,)), ((), ()))
TN = (((0,), (0,)), ((), ()))
VMEM = pl.BlockSpec(memory_space=pltpu.VMEM)
PARAMS = pltpu.CompilerParams(vmem_limit_bytes=60 * 1024 * 1024)


def dot(a, b, dims=(((1,), (0,)), ((), ()))):
    return lax.dot_general(a, b, dims, preferred_element_type=F32)


def slot_places(routing_ref, experts, capacity):
    tok = routing_ref.shape[1]
    ids = lax.broadcasted_iota(jnp.int32, (experts, tok), 0)
    first, second = routing_ref[0:1, :], routing_ref[1:2, :]
    hot0 = jnp.where(ids == first, 1.0, 0.0).astype(F32)
    hot1 = jnp.where(ids == second, 1.0, 0.0).astype(F32)
    row = lax.broadcasted_iota(jnp.int32, (tok, tok), 0)
    col = lax.broadcasted_iota(jnp.int32, (tok, tok), 1)
    before = jnp.where(row < col, 1.0, 0.0).astype(BF16)
    count0 = dot(hot0.astype(BF16), before)
    count1 = dot(hot1.astype(BF16), before) + jnp.sum(hot0, axis=1, keepdims=True)
    rank0 = jnp.sum(hot0 * count0, axis=0, keepdims=True).astype(jnp.int32)
    rank1 = jnp.sum(hot1 * count1, axis=0, keepdims=True).astype(jnp.int32)
    return first * capacity + rank0, second * capacity + rank1


def slot_masks(routing_ref, experts, capacity):
    tok = routing_ref.shape[1]
    place0, place1 = slot_places(routing_ref, experts, capacity)
    slots = lax.broadcasted_iota(jnp.int32, (experts * capacity, tok), 0)
    return (
        jnp.where(slots == place0, 1.0, 0.0).astype(BF16),
        jnp.where(slots == place1, 1.0, 0.0).astype(BF16),
    )


def build_x(experts, capacity, idx_ref, routing_ref, tok_ref, out_ref):
    mask0, mask1 = slot_masks(routing_ref, experts, capacity)
    half = tok_ref.shape[1] // 2
    for c in range(2):
        rows = dot(mask0 + mask1, tok_ref[:, c * half : (c + 1) * half])
        out_ref[:, c] = rows.astype(BF16).reshape(experts, capacity, half)


def build_g(experts, capacity, idx_ref, routing_ref, gates_ref, cot_ref, out_ref):
    mask0, mask1 = slot_masks(routing_ref, experts, capacity)
    half = cot_ref.shape[1] // 2
    for c in range(2):
        cot = cot_ref[:, c * half : (c + 1) * half].astype(F32)
        rows = dot(mask0, (gates_ref[:, 0:1] * cot).astype(BF16))
        rows = rows + dot(mask1, (gates_ref[:, 1:2] * cot).astype(BF16))
        out_ref[:, c] = rows.astype(BF16).reshape(experts, capacity, half)


def combine(experts, capacity, routing_ref, back_ref, out_ref):
    mask0, mask1 = slot_masks(routing_ref, experts, capacity)
    half = back_ref.shape[3]
    for c in range(2):
        rows = back_ref[:, c].reshape(experts * capacity, half)
        out_ref[:, c * half : (c + 1) * half] = dot(mask0 + mask1, rows, TN).astype(BF16)


def columns(idx_ref, place, width):
    return pl.ds(pl.multiple_of(idx_ref[place] * width, width), width)


def over_rows(total, tile, body):
    for half in range(2):

        @pl.loop(0, total // 2 // tile)
        def _(i, half=half):
            here = pl.multiple_of(i * tile, tile)
            body(half, pl.ds(pl.multiple_of(half * (total // 2) + here, tile), tile), pl.ds(here, tile))


def pick(refs, core, place, half):
    group = refs[core * 5 : core * 5 + 5]
    return group[place] if place < 3 else group[3 + half]


def gate_up(idx_ref, *refs):
    xs, (wg, wu, gate_ref, up_ref) = refs[:10], refs[10:]
    width = xs[0].shape[1]

    def body(half, rows, local):
        gate = up = None
        for core in range(2):
            for place in range(4):
                x = pick(xs, core, place, half)[rows if place < 3 else local, :]
                cols = columns(idx_ref, core * 4 + place, width)
                a, b = dot(x, wg[:, cols], NT), dot(x, wu[:, cols], NT)
                gate, up = (a, b) if gate is None else (gate + a, up + b)
        gate_ref[rows, :] = gate
        up_ref[rows, :] = up

    over_rows(xs[0].shape[0], 256, body)


def middle(idx_ref, *refs):
    gs, (wd, gate_ref, up_ref, hidden_ref, dgate_ref, dup_ref) = refs[:10], refs[10:]
    width = gs[0].shape[1]

    def body(half, rows, local):
        dhid = None
        for core in range(2):
            for place in range(4):
                g = pick(gs, core, place, half)[rows if place < 3 else local, :]
                a = dot(g, wd[:, columns(idx_ref, core * 4 + place, width)], NT)
                dhid = a if dhid is None else dhid + a
        gate, up = gate_ref[rows, :], up_ref[rows, :]
        sigma = jax.nn.sigmoid(gate)
        active = gate * sigma
        hidden_ref[rows, :] = (active * up).astype(BF16)
        dgate_ref[rows, :] = (dhid * up * sigma * (1.0 + gate * (1.0 - sigma))).astype(BF16)
        dup_ref[rows, :] = (dhid * active).astype(BF16)

    over_rows(gs[0].shape[0], 256, body)


def term_block(idx_ref, dgate_ref, dup_ref, wg, wu, out_ref):
    out_ref[0] = (dot(dgate_ref[...], wg[...]) + dot(dup_ref[...], wu[...])).astype(BF16)


def weight_grads(idx_ref, *refs):
    xs, gs, (hidden, dgate, dup, gg, ug, dg) = refs[:10], refs[10:20], refs[20:]
    width = xs[0].shape[1]
    rows = xs[0].shape[0]
    for core in range(2):
        for place in range(4):
            cols = columns(idx_ref, core * 4 + place, width)
            for left, right, out in ((dgate, xs, gg), (dup, xs, ug), (hidden, gs, dg)):
                if place < 3:
                    total = dot(left[...], right[core * 5 + place][...], TN)
                else:
                    total = dot(left[: rows // 2, :], right[core * 5 + 3][...], TN)
                    total = total + dot(left[rows // 2 :, :], right[core * 5 + 4][...], TN)
                out[:, cols] = total.astype(BF16)


def call(kernel, n_in, outs, *args, flops=0):
    moved = sum(a.size * a.dtype.itemsize for a in args) + sum(o.size * o.dtype.itemsize for o in outs)
    return pl.pallas_call(
        kernel,
        grid_spec=pltpu.PrefetchScalarGridSpec(
            num_scalar_prefetch=1, grid=(), in_specs=[VMEM] * n_in, out_specs=[VMEM] * len(outs)
        ),
        out_shape=outs,
        compiler_params=PARAMS,
        cost_estimate=pl.CostEstimate(flops=flops, bytes_accessed=moved, transcendentals=0),
    )(*args)


def per_device(tokens, cotangent, gates, routing, gate_weight, up_weight, down_weight):
    tok, width = tokens.shape
    n_exp, n_y = lax.axis_size("expert"), lax.axis_size("dp")
    experts = n_exp // 2
    capacity = 2 * tok * routing.shape[1] // experts
    rows = n_exp * capacity
    part = width // n_y
    block = part // 2
    hid = gate_weight.shape[1]
    y = lax.axis_index("dp").astype(jnp.int32)
    core = (lax.axis_index("expert") % 2).astype(jnp.int32)
    near = (y + jnp.array([0, n_y - 1, 1, 2], jnp.int32)) % n_y
    idx = jnp.concatenate([2 * near + core, 2 * near + (1 - core)])
    turn = [(i, (i + 1) % n_y) for i in range(n_y)]
    back_turn = [(i, (i - 1) % n_y) for i in range(n_y)]
    swap_pairs = [(i, i ^ 1) for i in range(n_exp)]

    def right(a):
        return lax.ppermute(a, "dp", turn)

    def left(a):
        return lax.ppermute(a, "dp", back_turn)

    def swap(a):
        return lax.ppermute(a, "expert", swap_pairs)

    def exchange(a):
        return lax.all_to_all(a, "expert", split_axis=0, concat_axis=0, tiled=True)

    wg, wu, wd = gate_weight[0], up_weight[0], down_weight[0]
    routes = routing.T
    yidx = y.reshape(1)

    def build(kernel, extra, data):
        return pl.pallas_call(
            functools.partial(kernel, experts, capacity),
            grid_spec=pltpu.PrefetchScalarGridSpec(
                num_scalar_prefetch=1,
                grid=(1,),
                in_specs=[pl.BlockSpec(a.shape, lambda i, s: (0, 0)) for a in (routes, *extra)]
                + [pl.BlockSpec((tok, part), lambda i, s: (0, s[0]))],
                out_specs=pl.BlockSpec((experts, 2, capacity, block), lambda i, s: (0, 0, 0, 0)),
            ),
            out_shape=jax.ShapeDtypeStruct((experts, 2, capacity, block), BF16),
            compiler_params=PARAMS,
        )(yidx, routes, *extra, data).reshape(n_exp, capacity, block)

    def spread(a):
        own = a.reshape(rows, block)
        p, m = right(own), left(own)
        q, r = right(p[: rows // 2]), left(m[rows // 2 :])
        mine = (own, p, m, q, r)
        return mine + tuple(swap(b) for b in mine)

    xs = spread(exchange(build(build_x, (), tokens)))
    gs = spread(exchange(build(build_g, (gates,), cotangent)))

    unit = 2 * rows * hid * width
    f32_mid = jax.ShapeDtypeStruct((rows, hid), F32)
    b16_mid = jax.ShapeDtypeStruct((rows, hid), BF16)
    gate, up = call(gate_up, 12, [f32_mid] * 2, idx, *xs, wg, wu, flops=2 * unit)
    hidden, dgate, dup = call(middle, 13, [b16_mid] * 3, idx, *gs, wd, gate, up, flops=unit)

    def terms(places):
        n = len(places)
        return pl.pallas_call(
            term_block,
            grid_spec=pltpu.PrefetchScalarGridSpec(
                num_scalar_prefetch=1,
                grid=(n,),
                in_specs=[pl.BlockSpec((rows, hid), lambda i, s: (0, 0))] * 2
                + [pl.BlockSpec((hid, block), lambda i, s: (0, s[i]))] * 2,
                out_specs=pl.BlockSpec((1, rows, block), lambda i, s: (i, 0, 0)),
            ),
            out_shape=jax.ShapeDtypeStruct((n, rows, block), BF16),
            compiler_params=PARAMS,
            cost_estimate=pl.CostEstimate(
                flops=unit // 4 * n, bytes_accessed=n * rows * block * 2, transcendentals=0
            ),
        )(idx[jnp.array(places, jnp.int32)], dgate, dup, wg, wu)

    def added(*parts):
        return sum(a.astype(F32) for a in parts)

    def over_cores(place):
        both = terms([4 + place, place])
        return both[1], swap(both[0])

    h = rows // 2
    a2, b2 = over_cores(3)
    opposite = added(a2, b2).astype(BF16)
    from_left, from_right = right(opposite[:h]), left(opposite[h:])
    a, b = over_cores(2)
    ahead0 = added(a[:h], b[:h], from_left).astype(BF16)
    ahead1 = added(a[h:], b[h:]).astype(BF16)
    a, b = over_cores(1)
    behind0 = added(a[:h], b[:h]).astype(BF16)
    behind1 = added(a[h:], b[h:], from_right).astype(BF16)
    got1, got2 = right(ahead1), left(behind0)
    got0, got3 = right(ahead0), left(behind1)
    a, b = over_cores(0)
    total = jnp.concatenate(
        [
            added(a[:h], b[:h], got0, got2).astype(BF16),
            added(a[h:], b[h:], got1, got3).astype(BF16),
        ]
    )
    back = exchange(total.reshape(n_exp, capacity, block))

    grads = call(
        weight_grads,
        23,
        [jax.ShapeDtypeStruct((hid, width), BF16)] * 3,
        idx,
        *xs,
        *gs,
        hidden,
        dgate,
        dup,
        flops=3 * unit,
    )
    input_grad = pl.pallas_call(
        functools.partial(combine, experts, capacity),
        in_specs=[VMEM] * 2,
        out_specs=VMEM,
        out_shape=jax.ShapeDtypeStruct((tok, part), BF16),
        compiler_params=PARAMS,
    )(routes, back.reshape(experts, 2, capacity, block))
    return (input_grad, grads[0][None], grads[1][None], grads[2][None])


def solution(mesh):
    weights = P("expert", "dp", None)
    return jax.shard_map(
        per_device,
        mesh=mesh,
        in_specs=(P("expert", None),) * 4 + (weights,) * 3,
        out_specs=(P("expert", "dp"),) + (weights,) * 3,
        check_vma=False,
    )
```

time: 723 us -> 268 us (0.37)
  waiting for transfers between devices: 530 us -> 133 us
  matrix products: 60.5 us -> 0 us
  Pallas kernels: 0 us -> 60.3 us
  other arithmetic: 30.5 us -> 2.86 us
  local copies, waits for them, and re-layouts: 46.9 us -> 19.3 us
  starting transfers between devices: 30.8 us -> 48.6 us
  between operations: 14.4 us -> 0.91 us
    all_to_all x3, waiting for transfers between devices: 520 us -> 60.4 us  [exchange(): return lax.all_to_all(a, 'expert', split_axis=0, concat_axis=0, tiled=True)]
    ppermute x0 -> x28, waiting for transfers between devices: none -> 72.3 us  [the longest x7 53.9 us: right(): return lax.ppermute(a, 'dp', turn)]
    dot_general x8 -> x0, matrix products: 60.5 us -> none  [the longest x1 11.3 us: owner_work(): terms = terms + jnp.dot(dup, w_up, preferred_element_type=jnp.float32)]
    pallas_call x0 -> x10, Pallas kernels: none -> 60.3 us  [the longest x3 34.4 us: call(): pl.pallas_call(kernel, grid_spec=pltpu.PrefetchScalarGridSpec(num_scalar_...]
    gather x4, local copies, waits for them, and re-layouts: 26.8 us -> 4.6 us  [terms(): idx[jnp.array(places, jnp.int32)]]
    ppermute x0 -> x28, starting transfers between devices: none -> 20.4 us  [the longest x14 7.49 us: swap(): return lax.ppermute(a, 'expert', swap_pairs)]
    reduce_sum x3 -> x0, other arithmetic: 18.4 us -> none  [the longest x1 9.43 us: per_device(): jnp.sum(back.reshape(experts, 2, capacity, width).astype(jnp.float32), ax...]
    broadcast_in_dim x3 -> x0, local copies, waits for them, and re-layouts: 10.8 us -> none  [the longest x1 6.48 us: per_device(): send_g = jnp.repeat(slot_g.reshape(experts, capacity, width), 2, axis=0)]
  transfers between devices with their start and end apart: 4 -> 31, of which waited for: 4 -> 14; matrix products, arithmetic and copies ran while one was open for 7% -> 6% of each run, Pallas kernels for 0% -> 16%
where the time goes in v1:
time: 268 us; the launch traced here: 265 us
  waiting for transfers between devices  133 us (50%)
  Pallas kernels  60.3 us (22%)
  starting transfers between devices  48.6 us (18%)
  local copies, waits for them, and re-layouts  19.3 us (7%)
  other arithmetic  2.86 us (1%)
    all_to_all x3, waiting for transfers between devices, exchange(): return lax.all_to_all(a, 'expert', split_axis=0, concat_axis=0, tiled=True)  60.4 us
    ppermute x7, waiting for transfers between devices, right(): return lax.ppermute(a, 'dp', turn)  53.9 us
    pallas_call x3, Pallas kernels, call(): pl.pallas_call(kernel, grid_spec=pltpu.PrefetchScalarGridSpec(num_scalar_...  34.4 us
    all_to_all x3, starting transfers between devices, exchange(): return lax.all_to_all(a, 'expert', split_axis=0, concat_axis=0, tiled=True)  28.2 us
    ppermute x7, waiting for transfers between devices, left(): return lax.ppermute(a, 'dp', back_turn)  18.4 us
    pallas_call x4, Pallas kernels, terms(): pl.pallas_call(term_block, grid_spec=pltpu.PrefetchScalarGridSpec(num_sca...  18.1 us
    squeeze x4, local copies, waits for them, and re-layouts, over_cores(): return (both[1], swap(both[0]))  8.26 us
    ppermute x14, starting transfers between devices, swap(): return lax.ppermute(a, 'expert', swap_pairs)  7.49 us
  transfers between devices with their start and end apart: 31, of which 14 were waited for; matrix products, arithmetic and copies ran while one was open for 6% of the time, Pallas kernels for 16%

profile of v1, /device:TPU:30, one launch (start us, length us, event | category | flops | bytes accessed | tf_op | source)
XLA Modules:
  0.0 264.7 jit_solution(7460125424870045401)
XLA Ops:
  0.6 2.5 shard_map.148
  3.1 12.4 %all-to-all-start.1 = ((bf16[64,16,512]{2,1,0:T(8,128)(2,1)}), bf16[64,16,512]{2,1,0:T(8,128)(2,1)}, u32[]{:S(2)}, u32[]{:S(2)}) async-start(bf16[64,16,512]{2,1,0:T(8,128)(2,1)} %bitcast.74), calls=%async_computation.1 | async-start | bytes 2097152 | tf_op jit(solution)/shard_map/all_to_all | solution.py:191
  16.3 2.8 %shard_map.147 = bf16[32,2,16,512]{3,2,1,0:T(8,128)(2,1)} custom-call(s32[1]{0:T(128)} %bitcast.1.idx_ref, s32[2,128]{1,0:T(2,128)} %bitcast.77, f32[128,2]{1,0:T(8,128)} %copy.17.gates_ref, bf16[128,4096]{1,0:T(8,128)(2,1)} %cot_ref.1), custom_call_target="tpu_custom_call" | custom-call | tf_op jit(solution)/shard_map/pallas_call | solution.py:198
  19.1 23.0 %all-to-all-done.1 = bf16[64,16,512]{2,1,0:T(8,128)(2,1)} async-done(((bf16[64,16,512]{2,1,0:T(8,128)(2,1)}), bf16[64,16,512]{2,1,0:T(8,128)(2,1)}, u32[]{:S(2)}, u32[]{:S(2)}) %all-to-all-start.1) | async-done | bytes 1048608 | tf_op jit(solution)/shard_map/all_to_all | solution.py:191
  42.1 8.1 %all-to-all-start = ((bf16[64,16,512]{2,1,0:T(8,128)(2,1)}), bf16[64,16,512]{2,1,0:T(8,128)(2,1)S(1)}, u32[]{:S(2)}, u32[]{:S(2)}) async-start(bf16[64,16,512]{2,1,0:T(8,128)(2,1)} %bitcast.73), calls=%async_computation | async-start | bytes 2097152 | tf_op jit(solution)/shard_map/all_to_all | solution.py:191
  50.5 1.8 collective-permute-start.10
  52.3 24.5 %all-to-all-done = bf16[64,16,512]{2,1,0:T(8,128)(2,1)S(1)} async-done(((bf16[64,16,512]{2,1,0:T(8,128)(2,1)}), bf16[64,16,512]{2,1,0:T(8,128)(2,1)S(1)}, u32[]{:S(2)}, u32[]{:S(2)}) %all-to-all-start) | async-done | bytes 1048608 | tf_op jit(solution)/shard_map/all_to_all | solution.py:191
  77.1 1.8 collective-permute-start.13
  78.8 1.6 collective-permute-start.1
  80.5 1.1 slice.117
  81.6 1.7 collective-permute-start.11
  83.2 1.1 slice.118
  84.8 17.1 %collective-permute-done.refs_1_.refs_11_ = bf16[1024,512]{1,0:T(8,128)(2,1)S(1)} collective-permute-done((bf16[1024,512]{1,0:T(8,128)(2,1)S(1)}, bf16[1024,512]{1,0:T(8,128)(2,1)S(1)}, u32[]{:S(2)}, u32[]{:S(2)}) %collective-permute-start) | collective-permute-done | bytes 1048608 | tf_op jit(solution)/shard_map/ppermute | solution.py:182
  102.0 1.4 collective-permute-start.2
  103.4 1.8 collective-permute-start.14
  106.1 7.1 %collective-permute-done.11.refs_3_ = bf16[512,512]{1,0:T(8,128)(2,1)S(1)} collective-permute-done((bf16[512,512]{1,0:T(8,128)(2,1)S(1)}, bf16[512,512]{1,0:T(8,128)(2,1)S(1)}, u32[]{:S(2)}, u32[]{:S(2)}) %collective-permute-start.11) | collective-permute-done | bytes 524320 | tf_op jit(solution)/shard_map/ppermute | solution.py:182
  113.9 2.5 collective-permute-done.12.refs_4_
  116.5 8.0 %collective-permute-done.2.refs_3_.refs_13_ = bf16[512,512]{1,0:T(8,128)(2,1)S(1)} collective-permute-done((bf16[512,512]{1,0:T(8,128)(2,1)S(1)}, bf16[512,512]{1,0:T(8,128)(2,1)S(1)}, u32[]{:S(2)}, u32[]{:S(2)}) %collective-permute-start.2) | collective-permute-done | bytes 524320 | tf_op jit(solution)/shard_map/ppermute | solution.py:182
  124.4 1.0 collective-permute-start.17
  125.5 2.7 %collective-permute-done.3.refs_4_.refs_14_ = bf16[512,512]{1,0:T(8,128)(2,1)S(1)} collective-permute-done((bf16[512,512]{1,0:T(8,128)(2,1)S(1)}, bf16[512,512]{1,0:T(8,128)(2,1)S(1)}, u32[]{:S(2)}, u32[]{:S(2)}) %collective-permute-start.3) | collective-permute-done | bytes 524320 | tf_op jit(solution)/shard_map/ppermute | solution.py:185
  131.5 1.1 gather_fusion.2
  132.7 11.4 %shard_map.149 = (f32[1024,192]{1,0:T(8,128)}, f32[1024,192]{1,0:T(8,128)}) custom-call(s32[8]{0:T(128)} %copy-done, bf16[1024,512]{1,0:T(8,128)(2,1)} %bitcast.6.refs_0_, bf16[1024,512]{1,0:T(8,128)(2,1)} %collective-permute-done.9.refs_1_, bf16[1024,512]{1,0:T(8,128)(2,1)} %collective-permute-done.10.refs_2_, bf16[512,512]{1,0:T(8,128)(2,1)} %copy-done.13, ...), custom_call_target="tpu_custom_call" | custom-call | flops 3221225472 | bytes 13107232 | tf_op jit(solution)/shard_map/pallas_call | solution.py:153
  144.1 9.2 %shard_map.150 = (bf16[1024,192]{1,0:T(8,128)(2,1)}, bf16[1024,192]{1,0:T(8,128)(2,1)}, bf16[1024,192]{1,0:T(8,128)(2,1)}) custom-call(s32[8]{0:T(128)} %copy-done, bf16[1024,512]{1,0:T(8,128)(2,1)} %bitcast.70, bf16[1024,512]{1,0:T(8,128)(2,1)} %copy-done.7, bf16[1024,512]{1,0:T(8,128)(2,1)} %copy-done.8, bf16[512,512]{1,0:T(8,128)(2,1)} %copy-done.10, ...), custom_call_target="tpu_custom_call" | custom-call | flops 1610612736 | bytes 12714016 | tf_op jit(solution)/shard_map/pallas_call | solution.py:153
  153.4 4.5 %shard_map.153 = bf16[2,1024,512]{2,1,0:T(8,128)(2,1)} custom-call(s32[2]{0:T(128)} %gather_fusion.2, bf16[1024,192]{1,0:T(8,128)(2,1)} %get-tuple-element.14.dgate_ref.refs_21_, bf16[1024,192]{1,0:T(8,128)(2,1)} %get-tuple-element.15.dup_ref.refs_22_, bf16[192,4096]{1,0:T(8,128)(2,1)} %bitcast.58, bf16[192,4096]{1,0:T(8,128)(2,1)} %bitcast.63), custom_call_target="tpu_custom_call" | custom-call | flops 805306368 | bytes 2097152 | tf_op jit(solution)/shard_map/pallas_call | solution.py:229
  157.9 2.3 slice_bitcast_fusion.1
  160.6 1.1 gather_fusion.1
  161.7 1.1 gather_fusion.3
  162.9 4.5 %shard_map.152 = bf16[2,1024,512]{2,1,0:T(8,128)(2,1)} custom-call(s32[2]{0:T(128)} %gather_fusion.1, bf16[1024,192]{1,0:T(8,128)(2,1)} %get-tuple-element.14.dgate_ref.refs_21_, bf16[1024,192]{1,0:T(8,128)(2,1)} %get-tuple-element.15.dup_ref.refs_22_, bf16[192,4096]{1,0:T(8,128)(2,1)} %bitcast.59, bf16[192,4096]{1,0:T(8,128)(2,1)} %bitcast.64), custom_call_target="tpu_custom_call" | custom-call | flops 805306368 | bytes 2097152 | tf_op jit(solution)/shard_map/pallas_call | solution.py:229
  167.4 2.3 slice_bitcast_fusion.3
  169.8 4.5 %shard_map.154 = bf16[2,1024,512]{2,1,0:T(8,128)(2,1)} custom-call(s32[2]{0:T(128)} %gather_fusion.3, bf16[1024,192]{1,0:T(8,128)(2,1)} %get-tuple-element.14.dgate_ref.refs_21_, bf16[1024,192]{1,0:T(8,128)(2,1)} %get-tuple-element.15.dup_ref.refs_22_, bf16[192,4096]{1,0:T(8,128)(2,1)} %bitcast.60, bf16[192,4096]{1,0:T(8,128)(2,1)} %bitcast.65), custom_call_target="tpu_custom_call" | custom-call | flops 805306368 | bytes 2097152 | tf_op jit(solution)/shard_map/pallas_call | solution.py:229
  174.4 2.4 slice_bitcast_fusion
  177.4 0.9 fusion.16
  178.5 1.2 gather_fusion
  179.7 4.5 %shard_map.151 = bf16[2,1024,512]{2,1,0:T(8,128)(2,1)} custom-call(s32[2]{0:T(128)} %gather_fusion, bf16[1024,192]{1,0:T(8,128)(2,1)} %get-tuple-element.14.dgate_ref.refs_21_, bf16[1024,192]{1,0:T(8,128)(2,1)} %get-tuple-element.15.dup_ref.refs_22_, bf16[192,4096]{1,0:T(8,128)(2,1)} %bitcast.61, bf16[192,4096]{1,0:T(8,128)(2,1)} %bitcast.66), custom_call_target="tpu_custom_call" | custom-call | flops 805306368 | bytes 2097152 | tf_op jit(solution)/shard_map/pallas_call | solution.py:229
  184.2 1.9 collective-permute-start.26
  186.1 1.3 slice_bitcast_fusion.4
  187.7 4.8 %collective-permute-done.21 = bf16[512,512]{1,0:T(8,128)(2,1)S(1)} collective-permute-done((bf16[512,512]{1,0:T(8,128)(2,1)}, bf16[512,512]{1,0:T(8,128)(2,1)S(1)}, u32[]{:S(2)}, u32[]{:S(2)}) %collective-permute-start.21) | collective-permute-done | bytes 524320 | tf_op jit(solution)/shard_map/ppermute | solution.py:182
  192.9 1.6 collective-permute-start.22
  194.6 4.7 %collective-permute-done.26 = bf16[512,512]{1,0:T(8,128)(2,1)S(1)} collective-permute-done((bf16[512,512]{1,0:T(8,128)(2,1)S(1)}, bf16[512,512]{1,0:T(8,128)(2,1)S(1)}, u32[]{:S(2)}, u32[]{:S(2)}) %collective-permute-start.26) | collective-permute-done | bytes 524320 | tf_op jit(solution)/shard_map/ppermute | solution.py:185
  200.5 7.3 %collective-permute-done.22 = bf16[512,512]{1,0:T(8,128)(2,1)S(1)} collective-permute-done((bf16[512,512]{1,0:T(8,128)(2,1)S(1)}, bf16[512,512]{1,0:T(8,128)(2,1)S(1)}, u32[]{:S(2)}, u32[]{:S(2)}) %collective-permute-start.22) | collective-permute-done | bytes 524320 | tf_op jit(solution)/shard_map/ppermute | solution.py:182
  207.9 9.6 %collective-permute-done.25 = bf16[512,512]{1,0:T(8,128)(2,1)S(1)} collective-permute-done((bf16[512,512]{1,0:T(8,128)(2,1)S(1)}, bf16[512,512]{1,0:T(8,128)(2,1)S(1)}, u32[]{:S(2)}, u32[]{:S(2)}) %collective-permute-start.25) | collective-permute-done | bytes 524320 | tf_op jit(solution)/shard_map/ppermute | solution.py:182
  217.4 7.7 %collective-permute-done.27 = bf16[512,512]{1,0:T(8,128)(2,1)S(1)} collective-permute-done((bf16[512,512]{1,0:T(8,128)(2,1)S(1)}, bf16[512,512]{1,0:T(8,128)(2,1)S(1)}, u32[]{:S(2)}, u32[]{:S(2)}) %collective-permute-start.27) | collective-permute-done | bytes 524320 | tf_op jit(solution)/shard_map/ppermute | solution.py:185
  225.7 1.1 pad_maximum_fusion
  226.8 7.7 %all-to-all-start.2 = ((bf16[64,16,512]{2,1,0:T(8,128)(2,1)}), bf16[64,16,512]{2,1,0:T(8,128)(2,1)S(1)}, u32[]{:S(2)}, u32[]{:S(2)}) async-start(bf16[64,16,512]{2,1,0:T(8,128)(2,1)} %bitcast.20), calls=%async_computation.2 | async-start | bytes 2097152 | tf_op jit(solution)/shard_map/all_to_all | solution.py:191
  234.5 13.8 %shard_map.156 = (bf16[192,4096]{1,0:T(8,128)(2,1)}, bf16[192,4096]{1,0:T(8,128)(2,1)}, bf16[192,4096]{1,0:T(8,128)(2,1)}) custom-call(s32[8]{0:T(128)} %copy-done, bf16[1024,512]{1,0:T(8,128)(2,1)} %bitcast.6.refs_0_, bf16[1024,512]{1,0:T(8,128)(2,1)} %collective-permute-done.9.refs_1_, bf16[1024,512]{1,0:T(8,128)(2,1)} %collective-permute-done.10.refs_2_, ...), custom_call_target="tpu_custom_call" | custom-call | flops 4831838208 | bytes 22675488 | tf_op jit(solution)/shard_map/pallas_call | solution.py:153
  248.3 12.9 %all-to-all-done.2 = bf16[64,16,512]{2,1,0:T(8,128)(2,1)S(1)} async-done(((bf16[64,16,512]{2,1,0:T(8,128)(2,1)}), bf16[64,16,512]{2,1,0:T(8,128)(2,1)S(1)}, u32[]{:S(2)}, u32[]{:S(2)}) %all-to-all-start.2) | async-done | bytes 1048608 | tf_op jit(solution)/shard_map/all_to_all | solution.py:191
  261.2 1.0 copy-done.9
  262.2 2.4 shard_map.155
  (96 shorter events, 10.8 us)
Async XLA Ops:
  0.6 14.9 %copy-start.17 = (f32[128,2]{0,1:T(2,128)S(1)}, f32[128,2]{0,1:T(2,128)}, u32[]{:S(2)}) copy-start(f32[128,2]{0,1:T(2,128)} %param.14) | copy-start | bytes 3076
  3.1 38.9 %all-to-all-start.1 = ((bf16[64,16,512]{2,1,0:T(8,128)(2,1)}), bf16[64,16,512]{2,1,0:T(8,128)(2,1)}, u32[]{:S(2)}, u32[]{:S(2)}) async-start(bf16[64,16,512]{2,1,0:T(8,128)(2,1)} %bitcast.74), calls=%async_computation.1 | async-start | bytes 2097152 | tf_op jit(solution)/shard_map/all_to_all | solution.py:191
  42.1 34.8 %all-to-all-start = ((bf16[64,16,512]{2,1,0:T(8,128)(2,1)}), bf16[64,16,512]{2,1,0:T(8,128)(2,1)S(1)}, u32[]{:S(2)}, u32[]{:S(2)}) async-start(bf16[64,16,512]{2,1,0:T(8,128)(2,1)} %bitcast.73), calls=%async_computation | async-start | bytes 2097152 | tf_op jit(solution)/shard_map/all_to_all | solution.py:191
  50.2 30.3 %collective-permute-start.9 = (bf16[1024,512]{1,0:T(8,128)(2,1)}, bf16[1024,512]{1,0:T(8,128)(2,1)}, u32[]{:S(2)}, u32[]{:S(2)}) collective-permute-start(bf16[1024,512]{1,0:T(8,128)(2,1)} %bitcast.6.refs_0_), channel_id=1, source_target_pairs={{0,1},{1,2},{2,3},{3,0},{4,5},{5,6},{6,7},{7,4},{8,9},{9,10},{10,1... | collective-permute-start | bytes 3145736 | tf_op jit(solution)/shard_map/ppermute | solution.py:182
  50.5 32.8 %collective-permute-start.10 = (bf16[1024,512]{1,0:T(8,128)(2,1)}, bf16[1024,512]{1,0:T(8,128)(2,1)}, u32[]{:S(2)}, u32[]{:S(2)}) collective-permute-start(bf16[1024,512]{1,0:T(8,128)(2,1)} %bitcast.6.refs_0_), channel_id=1, source_target_pairs={{0,3},{1,0},{2,1},{3,2},{4,7},{5,4},{6,5},{7,6},{8,11},{9,8},{10,9... | collective-permute-start | bytes 3145736 | tf_op jit(solution)/shard_map/ppermute | solution.py:185
  76.8 51.4 %copy-start.2 = (bf16[64,16,512]{2,1,0:T(8,128)(2,1)}, bf16[64,16,512]{2,1,0:T(8,128)(2,1)S(1)}, u32[]{:S(2)}) copy-start(bf16[64,16,512]{2,1,0:T(8,128)(2,1)S(1)} %all-to-all-done) | copy-start | bytes 3145732
  76.8 54.0 %copy-start.22 = (s32[4]{0:T(128)S(1)}, s32[4]{0:T(128)}, u32[]{:S(2)}) copy-start(s32[4]{0:T(128)} %constant.51.clone) | copy-start | bytes 52
  76.8 54.7 %copy-start.21 = (s32[2]{0:T(128)S(1)}, s32[2]{0:T(128)}, u32[]{:S(2)}) copy-start(s32[2]{0:T(128)} %constant.77) | copy-start | bytes 28
  76.8 25.1 %collective-permute-start = (bf16[1024,512]{1,0:T(8,128)(2,1)S(1)}, bf16[1024,512]{1,0:T(8,128)(2,1)S(1)}, u32[]{:S(2)}, u32[]{:S(2)}) collective-permute-start(bf16[1024,512]{1,0:T(8,128)(2,1)S(1)} %bitcast.67), channel_id=1, source_target_pairs={{0,1},{1,2},{2,3},{3,0},{4,5},{5,6},{6,7},{7,4},{8,9},{9,10},{10,1... | collective-permute-start | bytes 3145736 | tf_op jit(solution)/shard_map/ppermute | solution.py:182
  77.1 26.4 %collective-permute-start.13 = (bf16[1024,512]{1,0:T(8,128)(2,1)}, bf16[1024,512]{1,0:T(8,128)(2,1)S(1)}, u32[]{:S(2)}, u32[]{:S(2)}) collective-permute-start(bf16[1024,512]{1,0:T(8,128)(2,1)} %bitcast.6.refs_0_), channel_id=1, source_target_pairs={{0,4},{4,0},{8,12},{12,8},{16,20},{20,16},{24,28},{28,24},{32,36},... | collective-permute-start | bytes 3145736 | tf_op jit(solution)/shard_map/ppermute | solution.py:188
  78.8 27.2 %collective-permute-start.1 = (bf16[1024,512]{1,0:T(8,128)(2,1)S(1)}, bf16[1024,512]{1,0:T(8,128)(2,1)S(1)}, u32[]{:S(2)}, u32[]{:S(2)}) collective-permute-start(bf16[1024,512]{1,0:T(8,128)(2,1)S(1)} %bitcast.68), channel_id=1, source_target_pairs={{0,3},{1,0},{2,1},{3,2},{4,7},{5,4},{6,5},{7,6},{8,11},{9,8},{10,9... | collective-permute-start | bytes 3145736 | tf_op jit(solution)/shard_map/ppermute | solution.py:185
  81.6 31.6 %collective-permute-start.11 = (bf16[512,512]{1,0:T(8,128)(2,1)S(1)}, bf16[512,512]{1,0:T(8,128)(2,1)S(1)}, u32[]{:S(2)}, u32[]{:S(2)}) collective-permute-start(bf16[512,512]{1,0:T(8,128)(2,1)S(1)} %slice.117), channel_id=1, source_target_pairs={{0,1},{1,2},{2,3},{3,0},{4,5},{5,6},{6,7},{7,4},{8,9},{9,10},{10,1... | collective-permute-start | bytes 1572872 | tf_op jit(solution)/shard_map/ppermute | solution.py:182
  84.3 32.1 %collective-permute-start.12 = (bf16[512,512]{1,0:T(8,128)(2,1)S(1)}, bf16[512,512]{1,0:T(8,128)(2,1)S(1)}, u32[]{:S(2)}, u32[]{:S(2)}) collective-permute-start(bf16[512,512]{1,0:T(8,128)(2,1)S(1)} %slice.118), channel_id=1, source_target_pairs={{0,3},{1,0},{2,1},{3,2},{4,7},{5,4},{6,5},{7,6},{8,11},{9,8},{10,9... | collective-permute-start | bytes 1572872 | tf_op jit(solution)/shard_map/ppermute | solution.py:185
  101.9 42.1 %copy-start.7 = (bf16[1024,512]{1,0:T(8,128)(2,1)}, bf16[1024,512]{1,0:T(8,128)(2,1)S(1)}, u32[]{:S(2)}) copy-start(bf16[1024,512]{1,0:T(8,128)(2,1)S(1)} %collective-permute-done.refs_1_.refs_11_) | copy-start | bytes 3145732
  102.0 22.4 %collective-permute-start.2 = (bf16[512,512]{1,0:T(8,128)(2,1)S(1)}, bf16[512,512]{1,0:T(8,128)(2,1)S(1)}, u32[]{:S(2)}, u32[]{:S(2)}) collective-permute-start(bf16[512,512]{1,0:T(8,128)(2,1)S(1)} %slice.115), channel_id=1, source_target_pairs={{0,1},{1,2},{2,3},{3,0},{4,5},{5,6},{6,7},{7,4},{8,9},{9,10},{10,1... | collective-permute-start | bytes 1572872 | tf_op jit(solution)/shard_map/ppermute | solution.py:182
  103.4 25.7 %copy-start.12 = (bf16[1024,512]{1,0:T(8,128)(2,1)}, bf16[1024,512]{1,0:T(8,128)(2,1)S(1)}, u32[]{:S(2)}) copy-start(bf16[1024,512]{1,0:T(8,128)(2,1)S(1)} %collective-permute-done.13.refs_5_) | copy-start | bytes 3145732
  103.4 27.4 %collective-permute-start.14 = (bf16[1024,512]{1,0:T(8,128)(2,1)}, bf16[1024,512]{1,0:T(8,128)(2,1)}, u32[]{:S(2)}, u32[]{:S(2)}) collective-permute-start(bf16[1024,512]{1,0:T(8,128)(2,1)} %collective-permute-done.9.refs_1_), channel_id=1, source_target_pairs={{0,4},{4,0},{8,12},{12,8},{16,20},{20,16},{24,28},{28,24},{32,36},... | collective-permute-start | bytes 3145736 | tf_op jit(solution)/shard_map/ppermute | solution.py:188
  106.1 38.0 %copy-start.8 = (bf16[1024,512]{1,0:T(8,128)(2,1)}, bf16[1024,512]{1,0:T(8,128)(2,1)S(1)}, u32[]{:S(2)}) copy-start(bf16[1024,512]{1,0:T(8,128)(2,1)S(1)} %collective-permute-done.1.refs_2_.refs_12_) | copy-start | bytes 3145732
  106.1 25.2 %collective-permute-start.15 = (bf16[1024,512]{1,0:T(8,128)(2,1)}, bf16[1024,512]{1,0:T(8,128)(2,1)}, u32[]{:S(2)}, u32[]{:S(2)}) collective-permute-start(bf16[1024,512]{1,0:T(8,128)(2,1)} %collective-permute-done.10.refs_2_), channel_id=1, source_target_pairs={{0,4},{4,0},{8,12},{12,8},{16,20},{20,16},{24,28},{28,24},{32,36},... | collective-permute-start | bytes 3145736 | tf_op jit(solution)/shard_map/ppermute | solution.py:188
  113.2 16.0 %copy-start.13 = (bf16[512,512]{1,0:T(8,128)(2,1)}, bf16[512,512]{1,0:T(8,128)(2,1)S(1)}, u32[]{:S(2)}) copy-start(bf16[512,512]{1,0:T(8,128)(2,1)S(1)} %collective-permute-done.11.refs_3_) | copy-start | bytes 1572868
  113.2 15.0 %collective-permute-start.3 = (bf16[512,512]{1,0:T(8,128)(2,1)S(1)}, bf16[512,512]{1,0:T(8,128)(2,1)S(1)}, u32[]{:S(2)}, u32[]{:S(2)}) collective-permute-start(bf16[512,512]{1,0:T(8,128)(2,1)S(1)} %slice.116), channel_id=1, source_target_pairs={{0,3},{1,0},{2,1},{3,2},{4,7},{5,4},{6,5},{7,6},{8,11},{9,8},{10,9... | collective-permute-start | bytes 1572872 | tf_op jit(solution)/shard_map/ppermute | solution.py:185
  116.4 12.7 %copy-start.14 = (bf16[512,512]{1,0:T(8,128)(2,1)}, bf16[512,512]{1,0:T(8,128)(2,1)S(1)}, u32[]{:S(2)}) copy-start(bf16[512,512]{1,0:T(8,128)(2,1)S(1)} %collective-permute-done.12.refs_4_) | copy-start | bytes 1572868
  116.4 12.6 %collective-permute-start.16 = (bf16[512,512]{1,0:T(8,128)(2,1)S(1)}, bf16[512,512]{1,0:T(8,128)(2,1)S(1)}, u32[]{:S(2)}, u32[]{:S(2)}) collective-permute-start(bf16[512,512]{1,0:T(8,128)(2,1)S(1)} %collective-permute-done.11.refs_3_), channel_id=1, source_target_pairs={{0,4},{4,0},{8,12},{12,8},{16,20},{20,16},{24,28},{28,24},{32,36},... | collective-permute-start | bytes 1572872 | tf_op jit(solution)/shard_map/ppermute | solution.py:188
  124.4 4.7 %copy-start.10 = (bf16[512,512]{1,0:T(8,128)(2,1)}, bf16[512,512]{1,0:T(8,128)(2,1)S(1)}, u32[]{:S(2)}) copy-start(bf16[512,512]{1,0:T(8,128)(2,1)S(1)} %collective-permute-done.2.refs_3_.refs_13_) | copy-start | bytes 1572868
  124.4 4.7 %collective-permute-start.17 = (bf16[512,512]{1,0:T(8,128)(2,1)S(1)}, bf16[512,512]{1,0:T(8,128)(2,1)S(1)}, u32[]{:S(2)}, u32[]{:S(2)}) collective-permute-start(bf16[512,512]{1,0:T(8,128)(2,1)S(1)} %collective-permute-done.12.refs_4_), channel_id=1, source_target_pairs={{0,4},{4,0},{8,12},{12,8},{16,20},{20,16},{24,28},{28,24},{32,36},... | collective-permute-start | bytes 1572872 | tf_op jit(solution)/shard_map/ppermute | solution.py:188
  128.2 15.9 %collective-permute-start.4 = (bf16[1024,512]{1,0:T(8,128)(2,1)S(1)}, bf16[1024,512]{1,0:T(8,128)(2,1)}, u32[]{:S(2)}, u32[]{:S(2)}) collective-permute-start(bf16[1024,512]{1,0:T(8,128)(2,1)S(1)} %bitcast.69), channel_id=1, source_target_pairs={{0,4},{4,0},{8,12},{12,8},{16,20},{20,16},{24,28},{28,24},{32,36},... | collective-permute-start | bytes 3145736 | tf_op jit(solution)/shard_map/ppermute | solution.py:188
  129.0 15.1 %collective-permute-start.5 = (bf16[1024,512]{1,0:T(8,128)(2,1)S(1)}, bf16[1024,512]{1,0:T(8,128)(2,1)}, u32[]{:S(2)}, u32[]{:S(2)}) collective-permute-start(bf16[1024,512]{1,0:T(8,128)(2,1)S(1)} %collective-permute-done.refs_1_.refs_11_), channel_id=1, source_target_pairs={{0,4},{4,0},{8,12},{12,8},{16,20},{20,16},{24,28},{28,24},{32,36},... | collective-permute-start | bytes 3145736 | tf_op jit(solution)/shard_map/ppermute | solution.py:188
  130.7 13.5 %collective-permute-start.6 = (bf16[1024,512]{1,0:T(8,128)(2,1)S(1)}, bf16[1024,512]{1,0:T(8,128)(2,1)}, u32[]{:S(2)}, u32[]{:S(2)}) collective-permute-start(bf16[1024,512]{1,0:T(8,128)(2,1)S(1)} %collective-permute-done.1.refs_2_.refs_12_), channel_id=1, source_target_pairs={{0,4},{4,0},{8,12},{12,8},{16,20},{20,16},{24,28},{28,24},{32,36},... | collective-permute-start | bytes 3145736 | tf_op jit(solution)/shard_map/ppermute | solution.py:188
  130.9 13.2 %collective-permute-start.7 = (bf16[512,512]{1,0:T(8,128)(2,1)}, bf16[512,512]{1,0:T(8,128)(2,1)}, u32[]{:S(2)}, u32[]{:S(2)}) collective-permute-start(bf16[512,512]{1,0:T(8,128)(2,1)} %copy-done.10), channel_id=1, source_target_pairs={{0,4},{4,0},{8,12},{12,8},{16,20},{20,16},{24,28},{28,24},{32,36},... | collective-permute-start | bytes 1572872 | tf_op jit(solution)/shard_map/ppermute | solution.py:188
  131.3 12.8 %collective-permute-start.8 = (bf16[512,512]{1,0:T(8,128)(2,1)}, bf16[512,512]{1,0:T(8,128)(2,1)}, u32[]{:S(2)}, u32[]{:S(2)}) collective-permute-start(bf16[512,512]{1,0:T(8,128)(2,1)} %copy-done.11), channel_id=1, source_target_pairs={{0,4},{4,0},{8,12},{12,8},{16,20},{20,16},{24,28},{28,24},{32,36},... | collective-permute-start | bytes 1572872 | tf_op jit(solution)/shard_map/ppermute | solution.py:188
  157.9 2.7 %copy-start.20 = (s32[2]{0:T(128)S(1)}, s32[2]{0:T(128)}, u32[]{:S(2)}) copy-start(s32[2]{0:T(128)} %constant.76) | copy-start | bytes 28
  157.9 2.7 %copy-start.1 = (s32[8]{0:T(128)S(1)}, s32[8]{0:T(128)}, u32[]{:S(2)}) copy-start(s32[8]{0:T(128)} %copy-done) | copy-start | bytes 100
  157.9 3.8 %copy-start.19 = (s32[2]{0:T(128)S(1)}, s32[2]{0:T(128)}, u32[]{:S(2)}) copy-start(s32[2]{0:T(128)} %constant.78) | copy-start | bytes 28
  160.2 16.9 %collective-permute-start.20 = (bf16[1024,512]{1,0:T(8,128)(2,1)}, bf16[1024,512]{1,0:T(8,128)(2,1)S(1)}, u32[]{:S(2)}, u32[]{:S(2)}) collective-permute-start(bf16[1024,512]{1,0:T(8,128)(2,1)} %slice_bitcast_fusion.1), channel_id=1, source_target_pairs={{0,4},{4,0},{8,12},{12,8},{16,20},{20,16},{24,28},{28,24},{32,36},... | collective-permute-start | bytes 3145736 | tf_op jit(solution)/shard_map/ppermute | solution.py:188
  169.7 18.0 %collective-permute-start.19 = (bf16[1024,512]{1,0:T(8,128)(2,1)}, bf16[1024,512]{1,0:T(8,128)(2,1)S(1)}, u32[]{:S(2)}, u32[]{:S(2)}) collective-permute-start(bf16[1024,512]{1,0:T(8,128)(2,1)} %slice_bitcast_fusion.3), channel_id=1, source_target_pairs={{0,4},{4,0},{8,12},{12,8},{16,20},{20,16},{24,28},{28,24},{32,36},... | collective-permute-start | bytes 3145736 | tf_op jit(solution)/shard_map/ppermute | solution.py:188
  174.4 2.8 %copy-start.6 = (bf16[2,1024,512]{2,1,0:T(8,128)(2,1)S(1)}, bf16[2,1024,512]{2,1,0:T(8,128)(2,1)}, u32[]{:S(2)}) copy-start(bf16[2,1024,512]{2,1,0:T(8,128)(2,1)} %shard_map.153) | copy-start | bytes 6291460
  176.8 17.8 %collective-permute-start.23 = (bf16[1024,512]{1,0:T(8,128)(2,1)}, bf16[1024,512]{1,0:T(8,128)(2,1)S(1)}, u32[]{:S(2)}, u32[]{:S(2)}) collective-permute-start(bf16[1024,512]{1,0:T(8,128)(2,1)} %slice_bitcast_fusion), channel_id=1, source_target_pairs={{0,4},{4,0},{8,12},{12,8},{16,20},{20,16},{24,28},{28,24},{32,36},... | collective-permute-start | bytes 3145736 | tf_op jit(solution)/shard_map/ppermute | solution.py:188
  178.3 14.2 %collective-permute-start.21 = (bf16[512,512]{1,0:T(8,128)(2,1)}, bf16[512,512]{1,0:T(8,128)(2,1)S(1)}, u32[]{:S(2)}, u32[]{:S(2)}) collective-permute-start(bf16[512,512]{1,0:T(8,128)(2,1)} %get-tuple-element.28), channel_id=1, source_target_pairs={{0,1},{1,2},{2,3},{3,0},{4,5},{5,6},{6,7},{7,4},{8,9},{9,10},{10,1... | collective-permute-start | bytes 1572872 | tf_op jit(solution)/shard_map/ppermute | solution.py:182
  184.2 8.3 %copy-start.5 = (bf16[2,1024,512]{2,1,0:T(8,128)(2,1)S(1)}, bf16[2,1024,512]{2,1,0:T(8,128)(2,1)}, u32[]{:S(2)}) copy-start(bf16[2,1024,512]{2,1,0:T(8,128)(2,1)} %shard_map.152) | copy-start | bytes 6291460
  184.2 15.1 %collective-permute-start.26 = (bf16[512,512]{1,0:T(8,128)(2,1)S(1)}, bf16[512,512]{1,0:T(8,128)(2,1)S(1)}, u32[]{:S(2)}, u32[]{:S(2)}) collective-permute-start(bf16[512,512]{1,0:T(8,128)(2,1)S(1)} %get-tuple-element.29), channel_id=1, source_target_pairs={{0,3},{1,0},{2,1},{3,2},{4,7},{5,4},{6,5},{7,6},{8,11},{9,8},{10,9... | collective-permute-start | bytes 1572872 | tf_op jit(solution)/shard_map/ppermute | solution.py:185
  187.4 11.9 %copy-start.4 = (bf16[2,1024,512]{2,1,0:T(8,128)(2,1)S(1)}, bf16[2,1024,512]{2,1,0:T(8,128)(2,1)}, u32[]{:S(2)}) copy-start(bf16[2,1024,512]{2,1,0:T(8,128)(2,1)} %shard_map.154) | copy-start | bytes 6291460
  187.4 13.2 %collective-permute-start.18 = (bf16[1024,512]{1,0:T(8,128)(2,1)S(1)}, bf16[1024,512]{1,0:T(8,128)(2,1)S(1)}, u32[]{:S(2)}, u32[]{:S(2)}) collective-permute-start(bf16[1024,512]{1,0:T(8,128)(2,1)S(1)} %slice_bitcast_fusion.4), channel_id=1, source_target_pairs={{0,4},{4,0},{8,12},{12,8},{16,20},{20,16},{24,28},{28,24},{32,36},... | collective-permute-start | bytes 3145736 | tf_op jit(solution)/shard_map/ppermute | solution.py:188
  192.9 32.2 %copy-start.3 = (bf16[2,1024,512]{2,1,0:T(8,128)(2,1)S(1)}, bf16[2,1024,512]{2,1,0:T(8,128)(2,1)}, u32[]{:S(2)}) copy-start(bf16[2,1024,512]{2,1,0:T(8,128)(2,1)} %shard_map.151) | copy-start | bytes 6291460
  192.9 14.9 %collective-permute-start.22 = (bf16[512,512]{1,0:T(8,128)(2,1)S(1)}, bf16[512,512]{1,0:T(8,128)(2,1)S(1)}, u32[]{:S(2)}, u32[]{:S(2)}) collective-permute-start(bf16[512,512]{1,0:T(8,128)(2,1)S(1)} %get-tuple-element.24), channel_id=1, source_target_pairs={{0,1},{1,2},{2,3},{3,0},{4,5},{5,6},{6,7},{7,4},{8,9},{9,10},{10,1... | collective-permute-start | bytes 1572872 | tf_op jit(solution)/shard_map/ppermute | solution.py:182
  194.5 22.9 %collective-permute-start.25 = (bf16[512,512]{1,0:T(8,128)(2,1)S(1)}, bf16[512,512]{1,0:T(8,128)(2,1)S(1)}, u32[]{:S(2)}, u32[]{:S(2)}) collective-permute-start(bf16[512,512]{1,0:T(8,128)(2,1)S(1)} %get-tuple-element.25), channel_id=1, source_target_pairs={{0,1},{1,2},{2,3},{3,0},{4,5},{5,6},{6,7},{7,4},{8,9},{9,10},{10,1... | collective-permute-start | bytes 1572872 | tf_op jit(solution)/shard_map/ppermute | solution.py:182
  199.6 17.8 %collective-permute-start.24 = (bf16[512,512]{1,0:T(8,128)(2,1)S(1)}, bf16[512,512]{1,0:T(8,128)(2,1)S(1)}, u32[]{:S(2)}, u32[]{:S(2)}) collective-permute-start(bf16[512,512]{1,0:T(8,128)(2,1)S(1)} %get-tuple-element.26), channel_id=1, source_target_pairs={{0,3},{1,0},{2,1},{3,2},{4,7},{5,4},{6,5},{7,6},{8,11},{9,8},{10,9... | collective-permute-start | bytes 1572872 | tf_op jit(solution)/shard_map/ppermute | solution.py:185
  200.2 24.9 %collective-permute-start.27 = (bf16[512,512]{1,0:T(8,128)(2,1)S(1)}, bf16[512,512]{1,0:T(8,128)(2,1)S(1)}, u32[]{:S(2)}, u32[]{:S(2)}) collective-permute-start(bf16[512,512]{1,0:T(8,128)(2,1)S(1)} %get-tuple-element.27), channel_id=1, source_target_pairs={{0,3},{1,0},{2,1},{3,2},{4,7},{5,4},{6,5},{7,6},{8,11},{9,8},{10,9... | collective-permute-start | bytes 1572872 | tf_op jit(solution)/shard_map/ppermute | solution.py:185
  226.8 34.4 %all-to-all-start.2 = ((bf16[64,16,512]{2,1,0:T(8,128)(2,1)}), bf16[64,16,512]{2,1,0:T(8,128)(2,1)S(1)}, u32[]{:S(2)}, u32[]{:S(2)}) async-start(bf16[64,16,512]{2,1,0:T(8,128)(2,1)} %bitcast.20), calls=%async_computation.2 | async-start | bytes 2097152 | tf_op jit(solution)/shard_map/all_to_all | solution.py:191
  (6 other events, 6.5 us)

commit v2 on v0

v2 whole, which is shorter than its diff:
```python
import functools
import math

import jax
import jax.numpy as jnp
from jax import lax
from jax.experimental import pallas as pl
from jax.experimental.pallas import tpu as pltpu
from jax.sharding import PartitionSpec as P

F32 = jnp.float32
BF16 = jnp.bfloat16
NT = (((1,), (1,)), ((), ()))
TN = (((0,), (0,)), ((), ()))
MIB = 1024 * 1024


def dot(a, b, dims=(((1,), (0,)), ((), ()))):
    return lax.dot_general(a, b, dims, preferred_element_type=F32)


def slot_masks(routing_ref, experts, capacity):
    tok = routing_ref.shape[1]
    ids = lax.broadcasted_iota(jnp.int32, (experts, tok), 0)
    first, second = routing_ref[0:1, :], routing_ref[1:2, :]
    hot0 = jnp.where(ids == first, 1.0, 0.0).astype(F32)
    hot1 = jnp.where(ids == second, 1.0, 0.0).astype(F32)
    row = lax.broadcasted_iota(jnp.int32, (tok, tok), 0)
    col = lax.broadcasted_iota(jnp.int32, (tok, tok), 1)
    before = jnp.where(row < col, 1.0, 0.0).astype(BF16)
    count0 = dot(hot0.astype(BF16), before)
    count1 = dot(hot1.astype(BF16), before) + jnp.sum(hot0, axis=1, keepdims=True)
    rank0 = jnp.sum(hot0 * count0, axis=0, keepdims=True).astype(jnp.int32)
    rank1 = jnp.sum(hot1 * count1, axis=0, keepdims=True).astype(jnp.int32)
    slots = lax.broadcasted_iota(jnp.int32, (experts * capacity, tok), 0)
    return (
        jnp.where(slots == first * capacity + rank0, 1.0, 0.0).astype(BF16),
        jnp.where(slots == second * capacity + rank1, 1.0, 0.0).astype(BF16),
    )


def fetch_part(whole_ref, part_ref, sem):
    part = part_ref.shape[1]
    start = pl.multiple_of(lax.axis_index("dp") * part, part)
    return pltpu.make_async_copy(whole_ref.at[:, pl.ds(start, part)], part_ref, sem)


def build_x(experts, capacity, routing_ref, tok_ref, out_ref, part_ref, sem):
    copy = fetch_part(tok_ref, part_ref, sem)
    copy.start()
    mask0, mask1 = slot_masks(routing_ref, experts, capacity)
    copy.wait()
    out_ref[...] = dot(mask0 + mask1, part_ref[...]).astype(BF16)


def build_g(experts, capacity, routing_ref, gates_ref, cot_ref, out_ref, masks_ref, part_ref, sem):
    copy = fetch_part(cot_ref, part_ref, sem)
    copy.start()
    mask0, mask1 = slot_masks(routing_ref, experts, capacity)
    masks_ref[...] = (mask0 + mask1).astype(F32).T.astype(BF16)
    gates = gates_ref[...].T
    copy.wait()
    cot = part_ref[...].astype(F32)
    scaled = dot(mask0, (gates[:, 0:1] * cot).astype(BF16))
    scaled = scaled + dot(mask1, (gates[:, 1:2] * cot).astype(BF16))
    out_ref[...] = scaled.astype(BF16)


def combine(masks_ref, *refs):
    out_ref = refs[-1]
    half = refs[0].shape[1]
    for i, back_ref in enumerate(refs[:-1]):
        out_ref[:, i * half : (i + 1) * half] = dot(masks_ref[...], back_ref[...]).astype(BF16)


def columns(near_ref, place, width):
    return pl.ds(pl.multiple_of(near_ref[place] * width, width), width)


def gate_up(near_ref, *refs):
    xs, (wg, wu, gate_ref, up_ref) = refs[:10], refs[10:]
    rows, part = xs[0].shape
    h = rows // 2
    far = columns(near_ref, 3, part)
    for core in range(2):
        for w, out_ref in ((wg, gate_ref), (wu, up_ref)):
            total = None
            for place in range(3):
                a = dot(xs[core * 5 + place][...], w[:, columns(near_ref, place, part)], NT)
                total = a if place == 0 else total + a
            for half in range(2):
                here = slice(core * rows + half * h, core * rows + (half + 1) * h)
                out_ref[here, :] = total[half * h : (half + 1) * h] + dot(xs[core * 5 + 3 + half][...], w[:, far], NT)


def first_down(near_ref, *refs):
    gs, (wd, dhid_ref) = refs[:6], refs[6:]
    rows, part = gs[0].shape
    for core in range(2):
        dhid = None
        for place in range(3):
            a = dot(gs[core * 3 + place][...], wd[:, columns(near_ref, place, part)], NT)
            dhid = a if place == 0 else dhid + a
        dhid_ref[core * rows : (core + 1) * rows, :] = dhid


def last_products(near_ref, q, r, q_other, r_other, wd, gate_ref, up_ref, dhid_ref, hidden_ref, both_ref):
    h = q.shape[0]
    for i, g in enumerate((q, r, q_other, r_other)):
        here = slice(i * h, (i + 1) * h)
        gate, up = gate_ref[here, :], up_ref[here, :]
        dhid = dhid_ref[here, :] + dot(g[...], wd[...], NT)
        sigma = jax.nn.sigmoid(gate)
        active = gate * sigma
        hidden_ref[here, :] = (active * up).astype(BF16)
        dgate = (dhid * up * sigma * (1.0 + gate * (1.0 - sigma))).astype(BF16)
        dup = (dhid * active).astype(BF16)
        both_ref[here, :] = jnp.concatenate([dgate, dup], axis=1)


def term_block(near_ref, both_ref, wg, wu, mine_ref, theirs_ref):
    rows = mine_ref.shape[0]
    weights = jnp.concatenate([wg[...], wu[...]], axis=0)
    theirs_ref[...] = dot(both_ref[rows:, :], weights).astype(BF16)
    mine_ref[...] = dot(both_ref[:rows, :], weights).astype(BF16)


def near_blocks(near_ref, both_ref, *refs):
    for i in range(2):
        term_block(near_ref, both_ref, *refs[2 * i : 2 * i + 2], *refs[4 + 2 * i : 6 + 2 * i])


def cut(near_ref, p_ref, m_ref, x_ref, g_ref):
    x_ref[...] = p_ref[...]
    g_ref[...] = m_ref[...]


def plus(*refs):
    return sum(r[...].astype(F32) for r in refs)


def add_halves(near_ref, a_ref, b_ref, lo_ref, hi_ref):
    h = lo_ref.shape[0]
    total = plus(a_ref, b_ref).astype(BF16)
    lo_ref[...] = total[:h]
    hi_ref[...] = total[h:]


def add_beside(near_ref, a_ref, b_ref, lo_ref, c_ref, d_ref, hi_ref, *outs):
    h, part = lo_ref.shape
    for i in range(2):
        cols = slice(i * part // 2, (i + 1) * part // 2)
        for a, b, extra, at, out in ((a_ref, b_ref, lo_ref, 0, outs[i]), (c_ref, d_ref, hi_ref, 1, outs[2 + i])):
            for side in range(2):
                here = slice(side * h, (side + 1) * h)
                total = a[here, cols].astype(F32) + b[here, cols].astype(F32)
                if side == at:
                    total = total + extra[:, cols].astype(F32)
                out[here, :] = total.astype(BF16)


def add_last(near_ref, *refs):
    refs[-1][...] = plus(*refs[:-1]).astype(BF16)


def nothing(*refs):
    pass


def after(a, *others):
    anywhere = pl.BlockSpec(memory_space=pl.ANY)
    return pl.pallas_call(
        nothing,
        in_specs=[anywhere] * (1 + len(others)),
        out_specs=anywhere,
        out_shape=jax.ShapeDtypeStruct(a.shape, a.dtype),
        input_output_aliases={0: 0},
        compiler_params=pltpu.CompilerParams(vmem_limit_bytes=MIB),
        cost_estimate=pl.CostEstimate(flops=0, bytes_accessed=0, transcendentals=0),
    )(a, *others)


def weight_grads(near_ref, *refs):
    xs, gs, (hidden_ref, both_ref, gg, ug, dg) = refs[:10], refs[10:20], refs[20:]
    rows, part = xs[0].shape
    h = rows // 2
    hid = gg.shape[0]
    hidden, both = hidden_ref[...].T, both_ref[...].T
    for place in range(4):
        gate_up = down = None
        for core in range(2):
            for half in range(2):
                if place < 3 and half == 1:
                    continue
                at = core * 5 + place + half
                start = core * rows + half * h
                here = slice(start, start + xs[at].shape[0])
                a, b = dot(both[:, here], xs[at][...]), dot(hidden[:, here], gs[at][...])
                gate_up, down = (a, b) if gate_up is None else (gate_up + a, down + b)
        cols = columns(near_ref, place, part)
        gg[:, cols] = gate_up[:hid].astype(BF16)
        ug[:, cols] = gate_up[hid:].astype(BF16)
        dg[:, cols] = down.astype(BF16)


def call(kernel, near, args, outs, specs=None, deps=(), spare=10, flops=0):
    specs = specs or [None] * len(args)

    def spec(a, place=None):
        one = pl.Buffered(1)
        if place is None:
            return pl.BlockSpec(a.shape, lambda i, s: (0,) * len(a.shape), pipeline_mode=one)
        if isinstance(place, str):
            return pl.BlockSpec(
                (a.shape[0], a.shape[1] // 2), lambda i, s: (0, int(place)), pipeline_mode=one
            )
        if isinstance(place, tuple):
            return pl.BlockSpec(
                (a.shape[0] // place[1], a.shape[1]), lambda i, s: (place[0], 0), pipeline_mode=one
            )
        return pl.BlockSpec((a.shape[0], a.shape[1] // 4), lambda i, s: (0, s[place]), pipeline_mode=one)

    n = len(args)
    held = sum(math.prod(b.block_shape or a.shape) * a.dtype.itemsize for a, b in zip(args, map(spec, args, specs)))
    held += sum(o.size * o.dtype.itemsize for o in outs)

    def body(near_ref, *refs):
        kernel(near_ref, *refs[:n], *refs[n + len(deps) :])

    return pl.pallas_call(
        body,
        grid_spec=pltpu.PrefetchScalarGridSpec(
            num_scalar_prefetch=1,
            grid=(1,),
            in_specs=[spec(a, p) for a, p in zip(args, specs)] + [pl.BlockSpec(memory_space=pl.ANY)] * len(deps),
            out_specs=[spec(o) for o in outs],
        ),
        out_shape=outs,
        compiler_params=pltpu.CompilerParams(vmem_limit_bytes=held + spare * MIB),
        cost_estimate=pl.CostEstimate(flops=flops, bytes_accessed=0, transcendentals=0),
    )(near, *args, *deps)


def per_device(tokens, cotangent, gates, routing, gate_weight, up_weight, down_weight):
    tok, width = tokens.shape
    n_exp, n_y = lax.axis_size("expert"), lax.axis_size("dp")
    experts = n_exp // 2
    capacity = 2 * tok * routing.shape[1] // experts
    rows = experts * capacity
    part = width // n_y
    hid = gate_weight.shape[1]
    y = lax.axis_index("dp").astype(jnp.int32)
    near = (y + jnp.array([0, n_y - 1, 1, 2], jnp.int32)) % n_y
    turn = [(i, (i + 1) % n_y) for i in range(n_y)]
    back_turn = [(i, (i - 1) % n_y) for i in range(n_y)]
    swap_pairs = [(i, i ^ 1) for i in range(n_exp)]
    same_core = [list(range(c, n_exp, 2)) for c in range(2)]

    def right(a):
        return lax.ppermute(a, "dp", turn)

    def left(a):
        return lax.ppermute(a, "dp", back_turn)

    def swap(a):
        return lax.ppermute(a, "expert", swap_pairs)

    def exchange(a):
        shape = a.shape
        a = a.reshape(experts, capacity, shape[1])
        return lax.all_to_all(
            a, "expert", split_axis=0, concat_axis=0, tiled=True, axis_index_groups=same_core
        ).reshape(shape)

    def like(shape, dtype):
        return jax.ShapeDtypeStruct(shape, dtype)

    wg, wu, wd = gate_weight[0], up_weight[0], down_weight[0]
    routes = routing.T

    block = like((rows, part), BF16)
    half_block = like((rows // 2, part), BF16)
    vmem = pl.BlockSpec(memory_space=pltpu.VMEM)

    def slots(kernel, *args, outs):
        return pl.pallas_call(
            functools.partial(kernel, experts, capacity),
            in_specs=[vmem] * (len(args) - 1) + [pl.BlockSpec(memory_space=pl.ANY)],
            out_specs=[vmem] * len(outs),
            out_shape=outs,
            scratch_shapes=[pltpu.VMEM((tok, part), BF16), pltpu.SemaphoreType.DMA],
            compiler_params=pltpu.CompilerParams(vmem_limit_bytes=60 * MIB),
            cost_estimate=pl.CostEstimate(flops=0, bytes_accessed=0, transcendentals=0),
        )(*args)

    def cut_ends(p, m, flops=0):
        return call(cut, near, (p, m), [half_block] * 2, specs=[(0, 2), (1, 2)], flops=flops)

    x_sent = slots(build_x, routes, tokens, outs=[block])[0]
    x_own = exchange(x_sent)
    g_sent, masks = slots(build_g, routes, gates.T, cotangent, outs=[block, like((tok, rows), BF16)])
    x_own = after(x_own, g_sent)
    g_own = exchange(g_sent)

    x_p, x_m = right(x_own), left(x_own)
    x_q, x_r = cut_ends(x_p, x_m, flops=5 * 10**10)
    g_own = after(g_own, x_q)
    x_q, x_r = right(x_q), left(x_r)
    xs = (x_own, x_p, x_m, x_q, x_r)
    xs += tuple(swap(a) for a in xs)
    mids = call(gate_up, near, (*xs, wg, wu), [like((2 * rows, hid), F32)] * 2)

    g_p, g_m = right(g_own), left(g_own)
    g_first = (g_own, g_p, g_m)
    g_other = tuple(swap(a) for a in g_first)
    g_q, g_r = cut_ends(g_p, g_m)
    dhid = call(first_down, near, (*g_first, *g_other, wd), [like((2 * rows, hid), F32)], deps=mids[:1])[0]
    g_q, g_r = after(right(g_q), dhid), after(left(g_r), dhid)
    g_ends = (g_q, g_r, swap(g_q), swap(g_r))
    hidden, both = call(
        last_products,
        near,
        (*g_ends, wd, *mids, dhid),
        [like((2 * rows, hid), BF16), like((2 * rows, 2 * hid), BF16)],
        specs=[None] * 4 + [3] + [None] * 3,
    )

    side = like((rows, part // 2), BF16)
    far = call(term_block, near, (both, wg, wu), [block] * 2, specs=[None, 3, 3])
    beside = call(
        near_blocks, near, (both, *(wg, wu) * 2), [block] * 4, specs=[None, 2, 2, 1, 1], deps=far[:1]
    )
    lo, hi = call(add_halves, near, (far[0], swap(far[1])), [half_block] * 2, deps=beside[:1])
    own = call(term_block, near, (both, wg, wu), [block] * 2, specs=[None, 0, 0], deps=(lo,))
    sums = call(
        add_beside,
        near,
        (beside[0], swap(beside[1]), right(lo), beside[2], swap(beside[3]), left(hi)),
        [side] * 4,
    )
    own = (own[0], swap(own[1]))

    def total(i, deps=()):
        args = (*own, right(sums[i]), left(sums[2 + i]))
        return call(add_last, near, args, [side], specs=[str(i)] * 2 + [None] * 2, deps=deps, flops=10**12)[0]

    first = total(0)
    back = [exchange(first), exchange(total(1, (first,)))]
    grads = call(
        weight_grads,
        near,
        (*xs, *g_first, *g_ends[:2], *g_other, *g_ends[2:], hidden, both),
        [like((hid, width), BF16)] * 3,
        spare=38,
        flops=10**12,
    )
    input_grad = pl.pallas_call(
        combine,
        in_specs=[vmem] * 3,
        out_specs=vmem,
        out_shape=like((tok, part), BF16),
    )(masks, *back)
    return (input_grad, grads[0][None], grads[1][None], grads[2][None])


def solution(mesh):
    weights = P("expert", "dp", None)
    return jax.shard_map(
        per_device,
        mesh=mesh,
        in_specs=(P("expert", None),) * 4 + (weights,) * 3,
        out_specs=(P("expert", "dp"),) + (weights,) * 3,
        check_vma=False,
    )
```

time: 723 us -> 218 us (0.30); the launches traced: 714 us -> 217 us
  waiting for transfers between devices: 530 us -> 101 us
  matrix products: 60.5 us -> 0 us
  Pallas kernels: 0 us -> 50.7 us
  local copies, waits for them, and re-layouts: 46.9 us -> 0.09 us
  starting transfers between devices: 30.8 us -> 64.5 us
  other arithmetic: 30.5 us -> 0.01 us
  between operations: 14.4 us -> 1.13 us
    all_to_all x3 -> x4, waiting for transfers between devices: 520 us -> 40.2 us  [exchange(): lax.all_to_all(a, 'expert', split_axis=0, concat_axis=0, tiled=True, axis...]
    dot_general x8 -> x0, matrix products: 60.5 us -> none  [the longest x1 11.3 us: owner_work(): terms = terms + jnp.dot(dup, w_up, preferred_element_type=jnp.float32)]
    ppermute x0 -> x28, waiting for transfers between devices: none -> 60.4 us  [the longest x7 44.4 us: left(): return lax.ppermute(a, 'dp', back_turn)]
    pallas_call x0 -> x20, Pallas kernels: none -> 50.7 us  [the longest x13 42 us: call(): pl.pallas_call(body, grid_spec=pltpu.PrefetchScalarGridSpec(num_scalar_pr...]
    gather x4 -> x0, local copies, waits for them, and re-layouts: 26.8 us -> none  [the longest x1 9.92 us: per_device(): tokens[source_tok]]
    ppermute x0 -> x28, starting transfers between devices: none -> 24.9 us  [the longest x7 21.3 us: right(): return lax.ppermute(a, 'dp', turn)]
    reduce_sum x3 -> x0, other arithmetic: 18.4 us -> none  [the longest x1 9.43 us: per_device(): jnp.sum(back.reshape(experts, 2, capacity, width).astype(jnp.float32), ax...]
    broadcast_in_dim x3 -> x0, local copies, waits for them, and re-layouts: 10.8 us -> none  [the longest x1 6.48 us: per_device(): send_g = jnp.repeat(slot_g.reshape(experts, capacity, width), 2, axis=0)]
  transfers between devices with their start and end apart: 4 -> 32, of which waited for: 4 -> 13; matrix products, arithmetic and copies ran while one was open for 7% -> 0% of each run, Pallas kernels for 0% -> 19%
where the time goes in v2:
time: 218 us; the launch traced here: 217 us
  waiting for transfers between devices  101 us (46%)
  starting transfers between devices  64.5 us (30%)
  Pallas kernels  50.7 us (23%)
    ppermute x7, waiting for transfers between devices, left(): return lax.ppermute(a, 'dp', back_turn)  44.4 us
    pallas_call x13, Pallas kernels, call(): pl.pallas_call(body, grid_spec=pltpu.PrefetchScalarGridSpec(num_scalar_pr...  42 us
    all_to_all x4, waiting for transfers between devices, exchange(): lax.all_to_all(a, 'expert', split_axis=0, concat_axis=0, tiled=True, axis...  40.2 us
    all_to_all x4, starting transfers between devices, exchange(): lax.all_to_all(a, 'expert', split_axis=0, concat_axis=0, tiled=True, axis...  39.7 us
    ppermute x7, starting transfers between devices, right(): return lax.ppermute(a, 'dp', turn)  21.3 us
    ppermute x7, waiting for transfers between devices, right(): return lax.ppermute(a, 'dp', turn)  11.2 us
    pallas_call x2, Pallas kernels, slots(): pl.pallas_call(functools.partial(kernel, experts, capacity), in_specs=[vm...  6.44 us
    ppermute x14, waiting for transfers between devices, swap(): return lax.ppermute(a, 'expert', swap_pairs)  4.79 us
  transfers between devices with their start and end apart: 32, of which 13 were waited for; matrix products, arithmetic and copies ran while one was open for 0% of the time, Pallas kernels for 19%

profile of v2, /device:TPU:30, one launch (start us, length us, event | category | flops | bytes accessed | tf_op | source)
XLA Modules:
  0.0 217.0 jit_solution(6228169041165461993)
XLA Ops:
  0.6 3.0 %shard_map.112 = bf16[512,1024]{1,0:T(8,128)(2,1)} custom-call(s32[2,128]{1,0:T(2,128)} %bitcast.31, bf16[128,4096]{1,0:T(8,128)(2,1)} %tok_ref.1), custom_call_target="tpu_custom_call" | custom-call | tf_op jit(solution)/shard_map/pallas_call | solution.py:286
  3.7 11.6 %all-to-all-start.1 = ((bf16[32,16,1024]{2,1,0:T(8,128)(2,1)}), bf16[32,16,1024]{2,1,0:T(8,128)(2,1)S(1)}, u32[]{:S(2)}, u32[]{:S(2)}) async-start(bf16[32,16,1024]{2,1,0:T(8,128)(2,1)} %bitcast.30), calls=%async_computation.1 | async-start | bytes 2097152 | tf_op jit(solution)/shard_map/all_to_all | solution.py:271
  15.3 3.4 %shard_map.111 = (bf16[512,1024]{1,0:T(8,128)(2,1)}, bf16[128,512]{1,0:T(8,128)(2,1)}) custom-call(s32[2,128]{1,0:T(2,128)} %bitcast.32, f32[2,128]{1,0:T(2,128)} %bitcast.33, bf16[128,4096]{1,0:T(8,128)(2,1)} %cot_ref.1), custom_call_target="tpu_custom_call" | custom-call | tf_op jit(solution)/shard_map/pallas_call | solution.py:286
  18.7 23.0 %all-to-all-done.1 = bf16[32,16,1024]{2,1,0:T(8,128)(2,1)S(1)} async-done(((bf16[32,16,1024]{2,1,0:T(8,128)(2,1)}), bf16[32,16,1024]{2,1,0:T(8,128)(2,1)S(1)}, u32[]{:S(2)}, u32[]{:S(2)}) %all-to-all-start.1) | async-done | bytes 1048608 | tf_op jit(solution)/shard_map/all_to_all | solution.py:271
  41.7 0.7 collective-permute-start.1
  42.4 2.5 %collective-permute-start = (bf16[512,1024]{1,0:T(8,128)(2,1)S(1)}, bf16[512,1024]{1,0:T(8,128)(2,1)}, u32[]{:S(2)}, u32[]{:S(2)}) collective-permute-start(bf16[512,1024]{1,0:T(8,128)(2,1)S(1)} %shard_map.113.refs_0_), channel_id=1, source_target_pairs={{0,1},{1,2},{2,3},{3,0},{4,5},{5,6},{6,7},{7,4},{8,9},{9,10},{10,1... | collective-permute-start | bytes 3145736 | tf_op jit(solution)/shard_map/ppermute | solution.py:260
  44.9 7.3 %all-to-all-start = ((bf16[32,16,1024]{2,1,0:T(8,128)(2,1)}), bf16[32,16,1024]{2,1,0:T(8,128)(2,1)S(1)}, u32[]{:S(2)}, u32[]{:S(2)}) async-start(bf16[32,16,1024]{2,1,0:T(8,128)(2,1)} %bitcast.2), calls=%async_computation | async-start | bytes 2097152 | tf_op jit(solution)/shard_map/all_to_all | solution.py:271
  52.4 11.9 %collective-permute-done.1.refs_1_.refs_2_ = bf16[512,1024]{1,0:T(8,128)(2,1)S(1)} collective-permute-done((bf16[512,1024]{1,0:T(8,128)(2,1)S(1)}, bf16[512,1024]{1,0:T(8,128)(2,1)S(1)}, u32[]{:S(2)}, u32[]{:S(2)}) %collective-permute-start.1) | collective-permute-done | bytes 1048608 | tf_op jit(solution)/shard_map/ppermute | solution.py:263
  64.3 2.6 %shard_map.114 = (bf16[256,1024]{1,0:T(8,128)(2,1)}, bf16[256,1024]{1,0:T(8,128)(2,1)}) custom-call(s32[4]{0:T(128)S(1)} %and_select_fusion.near_ref, bf16[512,1024]{1,0:T(8,128)(2,1)} %collective-permute-done.refs_0_.refs_1_, bf16[512,1024]{1,0:T(8,128)(2,1)S(1)} %collective-permute-done.1.refs_1_.refs_2_), custom_call_target="tpu_custom_call" | custom-call | flops 49999998976 | tf_op jit(solution)/shard_map/pallas_call | solution.py:230
  66.9 3.2 %collective-permute-start.8 = (bf16[256,1024]{1,0:T(8,128)(2,1)}, bf16[256,1024]{1,0:T(8,128)(2,1)}, u32[]{:S(2)}, u32[]{:S(2)}) collective-permute-start(bf16[256,1024]{1,0:T(8,128)(2,1)} %get-tuple-element.33.refs_1_), channel_id=1, source_target_pairs={{0,1},{1,2},{2,3},{3,0},{4,5},{5,6},{6,7},{7,4},{8,9},{9,10},{10,1... | collective-permute-start | bytes 1572872 | tf_op jit(solution)/shard_map/ppermute | solution.py:260
  70.1 7.6 %all-to-all-done = bf16[32,16,1024]{2,1,0:T(8,128)(2,1)S(1)} async-done(((bf16[32,16,1024]{2,1,0:T(8,128)(2,1)}), bf16[32,16,1024]{2,1,0:T(8,128)(2,1)S(1)}, u32[]{:S(2)}, u32[]{:S(2)}) %all-to-all-start) | async-done | bytes 1048608 | tf_op jit(solution)/shard_map/all_to_all | solution.py:271
  77.8 3.2 %collective-permute-start.2 = (bf16[512,1024]{1,0:T(8,128)(2,1)S(1)}, bf16[512,1024]{1,0:T(8,128)(2,1)S(1)}, u32[]{:S(2)}, u32[]{:S(2)}) collective-permute-start(bf16[512,1024]{1,0:T(8,128)(2,1)S(1)} %shard_map.115.refs_0_.refs_10_), channel_id=1, source_target_pairs={{0,1},{1,2},{2,3},{3,0},{4,5},{5,6},{6,7},{7,4},{8,9},{9,10},{10,1... | collective-permute-start | bytes 3145736 | tf_op jit(solution)/shard_map/ppermute | solution.py:260
  81.1 0.5 collective-permute-start.13
  81.7 1.5 collective-permute-done.14.refs_9_
  83.2 0.1 collective-permute-start.11
  83.3 1.4 collective-permute-done.13.refs_8_
  84.8 15.2 %collective-permute-done.3.refs_1_.refs_2_.refs_12_ = bf16[512,1024]{1,0:T(8,128)(2,1)S(1)} collective-permute-done((bf16[512,1024]{1,0:T(8,128)(2,1)S(1)}, bf16[512,1024]{1,0:T(8,128)(2,1)S(1)}, u32[]{:S(2)}, u32[]{:S(2)}) %collective-permute-start.3) | collective-permute-done | bytes 1048608 | tf_op jit(solution)/shard_map/ppermute | solution.py:263
  100.0 0.5 collective-permute-start.6
  100.5 0.6 shard_map.116
  101.1 3.0 %collective-permute-start.4 = (bf16[256,1024]{1,0:T(8,128)(2,1)S(1)}, bf16[256,1024]{1,0:T(8,128)(2,1)S(1)}, u32[]{:S(2)}, u32[]{:S(2)}) collective-permute-start(bf16[256,1024]{1,0:T(8,128)(2,1)S(1)} %get-tuple-element.34), channel_id=1, source_target_pairs={{0,1},{1,2},{2,3},{3,0},{4,5},{5,6},{6,7},{7,4},{8,9},{9,10},{10,1... | collective-permute-start | bytes 1572872 | tf_op jit(solution)/shard_map/ppermute | solution.py:260
  104.2 7.2 %shard_map.117 = (f32[1024,192]{1,0:T(8,128)S(1)}, f32[1024,192]{1,0:T(8,128)S(1)}) custom-call(s32[4]{0:T(128)S(1)} %and_select_fusion.near_ref, bf16[512,1024]{1,0:T(8,128)(2,1)S(1)} %shard_map.113.refs_0_, bf16[512,1024]{1,0:T(8,128)(2,1)} %collective-permute-done.refs_0_.refs_1_, bf16[512,1024]{1,0:T(8,128)(2,1)S(1)} %collective-permute-done.1.refs_1_.refs_2_, ...), custom_call_target="tpu_custom_call" | custom-call | tf_op jit(solution)/shard_map/pallas_call | solution.py:230
  111.5 2.3 %shard_map.118.refs_1_.refs_7_ = f32[1024,192]{1,0:T(8,128)S(1)} custom-call(s32[4]{0:T(128)S(1)} %and_select_fusion.near_ref, bf16[512,1024]{1,0:T(8,128)(2,1)S(1)} %shard_map.115.refs_0_.refs_10_, bf16[512,1024]{1,0:T(8,128)(2,1)S(1)} %collective-permute-done.2.refs_0_.refs_1_.refs_11_, ...), custom_call_target="tpu_custom_call" | custom-call | tf_op jit(solution)/shard_map/pallas_call | solution.py:230
  113.9 2.1 collective-permute-done.4.refs_0_
  116.0 3.4 %collective-permute-done.15.refs_0_ = bf16[256,1024]{1,0:T(8,128)(2,1)S(1)} collective-permute-done((bf16[256,1024]{1,0:T(8,128)(2,1)S(1)}, bf16[256,1024]{1,0:T(8,128)(2,1)S(1)}, u32[]{:S(2)}, u32[]{:S(2)}) %collective-permute-start.15) | collective-permute-done | bytes 524320 | tf_op jit(solution)/shard_map/ppermute | solution.py:263
  119.4 1.9 collective-permute-done.17.refs_3_.refs_19_
  121.3 1.7 shard_map.121
  123.0 1.8 shard_map.122
  124.9 0.2 collective-permute-start.18
  125.1 2.9 %shard_map.123 = (bf16[512,1024]{1,0:T(8,128)(2,1)S(1)}, bf16[512,1024]{1,0:T(8,128)(2,1)S(1)}, bf16[512,1024]{1,0:T(8,128)(2,1)S(1)}, bf16[512,1024]{1,0:T(8,128)(2,1)S(1)}) custom-call(s32[4]{0:T(128)S(1)} %and_select_fusion.near_ref, bf16[1024,384]{1,0:T(8,128)(2,1)S(1)} %get-tuple-element.39.refs_0_.refs_21_, bf16[192,4096]{1,0:T(8,128)(2,1)S(1)} %bitcast.18, ...), custom_call_target="tpu_custom_call" | custom-call | tf_op jit(solution)/shard_map/pallas_call | solution.py:230
  128.0 0.5 collective-permute-start.20
  128.4 0.1 collective-permute-start.22
  128.6 0.8 shard_map.124
  129.4 0.3 collective-permute-start.23
  129.7 3.2 %collective-permute-start.21 = (bf16[256,1024]{1,0:T(8,128)(2,1)S(1)}, bf16[256,1024]{1,0:T(8,128)(2,1)S(1)}, u32[]{:S(2)}, u32[]{:S(2)}) collective-permute-start(bf16[256,1024]{1,0:T(8,128)(2,1)S(1)} %get-tuple-element.43.refs_3_), channel_id=1, source_target_pairs={{0,1},{1,2},{2,3},{3,0},{4,5},{5,6},{6,7},{7,4},{8,9},{9,10},{10,1... | collective-permute-start | bytes 1572872 | tf_op jit(solution)/shard_map/ppermute | solution.py:260
  132.9 1.8 shard_map.125
  134.8 10.2 %collective-permute-done.23.refs_5_ = bf16[256,1024]{1,0:T(8,128)(2,1)S(1)} collective-permute-done((bf16[256,1024]{1,0:T(8,128)(2,1)S(1)}, bf16[256,1024]{1,0:T(8,128)(2,1)S(1)}, u32[]{:S(2)}, u32[]{:S(2)}) %collective-permute-start.23) | collective-permute-done | bytes 524320 | tf_op jit(solution)/shard_map/ppermute | solution.py:263
  145.1 1.9 shard_map.126
  147.0 3.0 %collective-permute-start.24 = (bf16[512,512]{1,0:T(8,128)(2,1)S(1)}, bf16[512,512]{1,0:T(8,128)(2,1)S(1)}, u32[]{:S(2)}, u32[]{:S(2)}) collective-permute-start(bf16[512,512]{1,0:T(8,128)(2,1)S(1)} %get-tuple-element.50), channel_id=1, source_target_pairs={{0,1},{1,2},{2,3},{3,0},{4,5},{5,6},{6,7},{7,4},{8,9},{9,10},{10,1... | collective-permute-start | bytes 1572872 | tf_op jit(solution)/shard_map/ppermute | solution.py:260
  149.9 3.2 %collective-permute-start.26 = (bf16[512,512]{1,0:T(8,128)(2,1)}, bf16[512,512]{1,0:T(8,128)(2,1)}, u32[]{:S(2)}, u32[]{:S(2)}) collective-permute-start(bf16[512,512]{1,0:T(8,128)(2,1)} %get-tuple-element.52), channel_id=1, source_target_pairs={{0,1},{1,2},{2,3},{3,0},{4,5},{5,6},{6,7},{7,4},{8,9},{9,10},{10,1... | collective-permute-start | bytes 1572872 | tf_op jit(solution)/shard_map/ppermute | solution.py:260
  153.2 9.1 %collective-permute-done.24.refs_2_ = bf16[512,512]{1,0:T(8,128)(2,1)S(1)} collective-permute-done((bf16[512,512]{1,0:T(8,128)(2,1)S(1)}, bf16[512,512]{1,0:T(8,128)(2,1)S(1)}, u32[]{:S(2)}, u32[]{:S(2)}) %collective-permute-start.24) | collective-permute-done | bytes 524320 | tf_op jit(solution)/shard_map/ppermute | solution.py:260
  162.3 3.7 %collective-permute-done.25.refs_3_ = bf16[512,512]{1,0:T(8,128)(2,1)S(1)} collective-permute-done((bf16[512,512]{1,0:T(8,128)(2,1)S(1)}, bf16[512,512]{1,0:T(8,128)(2,1)S(1)}, u32[]{:S(2)}, u32[]{:S(2)}) %collective-permute-start.25) | collective-permute-done | bytes 524320 | tf_op jit(solution)/shard_map/ppermute | solution.py:263
  166.0 1.6 shard_map.127.refs_4_
  167.6 13.9 %all-to-all-start.2 = ((bf16[32,16,512]{2,1,0:T(8,128)(2,1)}), bf16[32,16,512]{2,1,0:T(8,128)(2,1)}, u32[]{:S(2)}, u32[]{:S(2)}) async-start(bf16[32,16,512]{2,1,0:T(8,128)(2,1)} %bitcast.9), calls=%async_computation.2 | async-start | bytes 1048576 | tf_op jit(solution)/shard_map/all_to_all | solution.py:271
  181.6 2.9 %shard_map.128 = bf16[512,512]{1,0:T(8,128)(2,1)} custom-call(s32[4]{0:T(128)S(1)} %and_select_fusion.near_ref, bf16[512,1024]{1,0:T(8,128)(2,1)S(1)} %get-tuple-element.44.refs_0_, bf16[512,1024]{1,0:T(8,128)(2,1)S(1)} %collective-permute-done.19.refs_1_, bf16[512,512]{1,0:T(8,128)(2,1)} %collective-permute-done.26.refs_2_, ...), custom_call_target="tpu_custom_call" | custom-call | flops 999999995904 | tf_op jit(solution)/shard_map/pallas_call | solution.py:230
  184.4 9.6 %all-to-all-done.2 = bf16[32,16,512]{2,1,0:T(8,128)(2,1)} async-done(((bf16[32,16,512]{2,1,0:T(8,128)(2,1)}), bf16[32,16,512]{2,1,0:T(8,128)(2,1)}, u32[]{:S(2)}, u32[]{:S(2)}) %all-to-all-start.2) | async-done | bytes 524320 | tf_op jit(solution)/shard_map/all_to_all | solution.py:271
  194.0 6.8 %all-to-all-start.3 = ((bf16[32,16,512]{2,1,0:T(8,128)(2,1)}), bf16[32,16,512]{2,1,0:T(8,128)(2,1)}, u32[]{:S(2)}, u32[]{:S(2)}) async-start(bf16[32,16,512]{2,1,0:T(8,128)(2,1)} %bitcast.11), calls=%async_computation.3 | async-start | bytes 1048576 | tf_op jit(solution)/shard_map/all_to_all | solution.py:271
  200.8 13.9 %shard_map.130 = (bf16[192,4096]{1,0:T(8,128)(2,1)}, bf16[192,4096]{1,0:T(8,128)(2,1)}, bf16[192,4096]{1,0:T(8,128)(2,1)}) custom-call(s32[4]{0:T(128)} %copy-done.20, bf16[512,1024]{1,0:T(8,128)(2,1)} %copy-done.2, bf16[512,1024]{1,0:T(8,128)(2,1)} %collective-permute-done.refs_0_.refs_1_, bf16[512,1024]{1,0:T(8,128)(2,1)} %copy-done.10, ...), custom_call_target="tpu_custom_call" | custom-call | flops 999999995904 | tf_op jit(solution)/shard_map/pallas_call | solution.py:230
  214.7 2.3 %shard_map.129 = bf16[128,1024]{1,0:T(8,128)(2,1)} custom-call(bf16[128,512]{1,0:T(8,128)(2,1)} %get-tuple-element.31.masks_ref, bf16[512,512]{1,0:T(8,128)(2,1)} %bitcast.10.refs_0_, bf16[512,512]{1,0:T(8,128)(2,1)} %bitcast.12.refs_1_), custom_call_target="tpu_custom_call" | custom-call | tf_op jit(solution)/shard_map/pallas_call | solution.py:357
  (83 shorter events, 0.7 us)
Async XLA Ops:
  3.7 38.0 %all-to-all-start.1 = ((bf16[32,16,1024]{2,1,0:T(8,128)(2,1)}), bf16[32,16,1024]{2,1,0:T(8,128)(2,1)S(1)}, u32[]{:S(2)}, u32[]{:S(2)}) async-start(bf16[32,16,1024]{2,1,0:T(8,128)(2,1)} %bitcast.30), calls=%async_computation.1 | async-start | bytes 2097152 | tf_op jit(solution)/shard_map/all_to_all | solution.py:271
  41.7 62.4 %copy-start.2 = (bf16[512,1024]{1,0:T(8,128)(2,1)}, bf16[512,1024]{1,0:T(8,128)(2,1)S(1)}, u32[]{:S(2)}) copy-start(bf16[512,1024]{1,0:T(8,128)(2,1)S(1)} %shard_map.113.refs_0_) | copy-start | bytes 3145732
  41.7 10.6 %copy-start.22 = (s32[4]{0:T(128)S(1)}, s32[4]{0:T(128)}, u32[]{:S(2)}) copy-start(s32[4]{0:T(128)} %constant.21.clone) | copy-start | bytes 52
  41.7 22.6 %collective-permute-start.1 = (bf16[512,1024]{1,0:T(8,128)(2,1)S(1)}, bf16[512,1024]{1,0:T(8,128)(2,1)S(1)}, u32[]{:S(2)}, u32[]{:S(2)}) collective-permute-start(bf16[512,1024]{1,0:T(8,128)(2,1)S(1)} %shard_map.113.refs_0_), channel_id=1, source_target_pairs={{0,3},{1,0},{2,1},{3,2},{4,7},{5,4},{6,5},{7,6},{8,11},{9,8},{10,9... | collective-permute-start | bytes 3145736 | tf_op jit(solution)/shard_map/ppermute | solution.py:263
  42.4 21.8 %collective-permute-start = (bf16[512,1024]{1,0:T(8,128)(2,1)S(1)}, bf16[512,1024]{1,0:T(8,128)(2,1)}, u32[]{:S(2)}, u32[]{:S(2)}) collective-permute-start(bf16[512,1024]{1,0:T(8,128)(2,1)S(1)} %shard_map.113.refs_0_), channel_id=1, source_target_pairs={{0,1},{1,2},{2,3},{3,0},{4,5},{5,6},{6,7},{7,4},{8,9},{9,10},{10,1... | collective-permute-start | bytes 3145736 | tf_op jit(solution)/shard_map/ppermute | solution.py:260
  44.9 32.8 %all-to-all-start = ((bf16[32,16,1024]{2,1,0:T(8,128)(2,1)}), bf16[32,16,1024]{2,1,0:T(8,128)(2,1)S(1)}, u32[]{:S(2)}, u32[]{:S(2)}) async-start(bf16[32,16,1024]{2,1,0:T(8,128)(2,1)} %bitcast.2), calls=%async_computation | async-start | bytes 2097152 | tf_op jit(solution)/shard_map/all_to_all | solution.py:271
  52.3 129.3 %copy-start.20 = (s32[4]{0:T(128)}, s32[4]{0:T(128)S(1)}, u32[]{:S(2)}) copy-start(s32[4]{0:T(128)S(1)} %and_select_fusion.near_ref) | copy-start | bytes 52
  52.3 29.3 %collective-permute-start.10 = (bf16[512,1024]{1,0:T(8,128)(2,1)S(1)}, bf16[512,1024]{1,0:T(8,128)(2,1)}, u32[]{:S(2)}, u32[]{:S(2)}) collective-permute-start(bf16[512,1024]{1,0:T(8,128)(2,1)S(1)} %shard_map.113.refs_0_), channel_id=1, source_target_pairs={{0,4},{4,0},{8,12},{12,8},{16,20},{20,16},{24,28},{28,24},{32,36},... | collective-permute-start | bytes 3145736 | tf_op jit(solution)/shard_map/ppermute | solution.py:266
  64.3 39.9 %copy-start.10 = (bf16[512,1024]{1,0:T(8,128)(2,1)}, bf16[512,1024]{1,0:T(8,128)(2,1)S(1)}, u32[]{:S(2)}) copy-start(bf16[512,1024]{1,0:T(8,128)(2,1)S(1)} %collective-permute-done.1.refs_1_.refs_2_) | copy-start | bytes 3145732
  66.9 14.2 %collective-permute-start.9 = (bf16[256,1024]{1,0:T(8,128)(2,1)}, bf16[256,1024]{1,0:T(8,128)(2,1)}, u32[]{:S(2)}, u32[]{:S(2)}) collective-permute-start(bf16[256,1024]{1,0:T(8,128)(2,1)} %get-tuple-element.35), channel_id=1, source_target_pairs={{0,3},{1,0},{2,1},{3,2},{4,7},{5,4},{6,5},{7,6},{8,11},{9,8},{10,9... | collective-permute-start | bytes 1572872 | tf_op jit(solution)/shard_map/ppermute | solution.py:263
  66.9 14.2 %collective-permute-start.8 = (bf16[256,1024]{1,0:T(8,128)(2,1)}, bf16[256,1024]{1,0:T(8,128)(2,1)}, u32[]{:S(2)}, u32[]{:S(2)}) collective-permute-start(bf16[256,1024]{1,0:T(8,128)(2,1)} %get-tuple-element.33.refs_1_), channel_id=1, source_target_pairs={{0,1},{1,2},{2,3},{3,0},{4,5},{5,6},{6,7},{7,4},{8,9},{9,10},{10,1... | collective-permute-start | bytes 1572872 | tf_op jit(solution)/shard_map/ppermute | solution.py:260
  77.7 26.4 %copy-start.1 = (bf16[1,192,4096]{2,1,0:T(8,128)(2,1)S(1)}, bf16[1,192,4096]{2,1,0:T(8,128)(2,1)}, u32[]{:S(2)}) copy-start(bf16[1,192,4096]{2,1,0:T(8,128)(2,1)} %param.13) | copy-start | bytes 4718596
  77.7 33.7 %copy-start.3 = (bf16[512,1024]{1,0:T(8,128)(2,1)}, bf16[512,1024]{1,0:T(8,128)(2,1)S(1)}, u32[]{:S(2)}) copy-start(bf16[512,1024]{1,0:T(8,128)(2,1)S(1)} %shard_map.115.refs_0_.refs_10_) | copy-start | bytes 3145732
  77.7 26.4 %copy-start = (bf16[1,192,4096]{2,1,0:T(8,128)(2,1)S(1)}, bf16[1,192,4096]{2,1,0:T(8,128)(2,1)}, u32[]{:S(2)}) copy-start(bf16[1,192,4096]{2,1,0:T(8,128)(2,1)} %param.12) | copy-start | bytes 4718596
  77.7 22.2 %collective-permute-start.3 = (bf16[512,1024]{1,0:T(8,128)(2,1)S(1)}, bf16[512,1024]{1,0:T(8,128)(2,1)S(1)}, u32[]{:S(2)}, u32[]{:S(2)}) collective-permute-start(bf16[512,1024]{1,0:T(8,128)(2,1)S(1)} %shard_map.115.refs_0_.refs_10_), channel_id=1, source_target_pairs={{0,3},{1,0},{2,1},{3,2},{4,7},{5,4},{6,5},{7,6},{8,11},{9,8},{10,9... | collective-permute-start | bytes 3145736 | tf_op jit(solution)/shard_map/ppermute | solution.py:263
  77.8 22.2 %collective-permute-start.2 = (bf16[512,1024]{1,0:T(8,128)(2,1)S(1)}, bf16[512,1024]{1,0:T(8,128)(2,1)S(1)}, u32[]{:S(2)}, u32[]{:S(2)}) collective-permute-start(bf16[512,1024]{1,0:T(8,128)(2,1)S(1)} %shard_map.115.refs_0_.refs_10_), channel_id=1, source_target_pairs={{0,1},{1,2},{2,3},{3,0},{4,5},{5,6},{6,7},{7,4},{8,9},{9,10},{10,1... | collective-permute-start | bytes 3145736 | tf_op jit(solution)/shard_map/ppermute | solution.py:260
  81.1 2.1 collective-permute-start.14
  81.1 3.6 %collective-permute-start.13 = (bf16[256,1024]{1,0:T(8,128)(2,1)}, bf16[256,1024]{1,0:T(8,128)(2,1)S(1)}, u32[]{:S(2)}, u32[]{:S(2)}) collective-permute-start(bf16[256,1024]{1,0:T(8,128)(2,1)} %collective-permute-done.8.refs_3_), channel_id=1, source_target_pairs={{0,4},{4,0},{8,12},{12,8},{16,20},{20,16},{24,28},{28,24},{32,36},... | collective-permute-start | bytes 1572872 | tf_op jit(solution)/shard_map/ppermute | solution.py:266
  81.6 19.5 %collective-permute-start.12 = (bf16[512,1024]{1,0:T(8,128)(2,1)S(1)}, bf16[512,1024]{1,0:T(8,128)(2,1)S(1)}, u32[]{:S(2)}, u32[]{:S(2)}) collective-permute-start(bf16[512,1024]{1,0:T(8,128)(2,1)S(1)} %collective-permute-done.1.refs_1_.refs_2_), channel_id=1, source_target_pairs={{0,4},{4,0},{8,12},{12,8},{16,20},{20,16},{24,28},{28,24},{32,36},... | collective-permute-start | bytes 3145736 | tf_op jit(solution)/shard_map/ppermute | solution.py:266
  83.2 28.2 %copy-start.16 = (bf16[256,1024]{1,0:T(8,128)(2,1)}, bf16[256,1024]{1,0:T(8,128)(2,1)S(1)}, u32[]{:S(2)}) copy-start(bf16[256,1024]{1,0:T(8,128)(2,1)S(1)} %collective-permute-done.14.refs_9_) | copy-start | bytes 1572868
  83.2 20.9 %collective-permute-start.11 = (bf16[512,1024]{1,0:T(8,128)(2,1)}, bf16[512,1024]{1,0:T(8,128)(2,1)S(1)}, u32[]{:S(2)}, u32[]{:S(2)}) collective-permute-start(bf16[512,1024]{1,0:T(8,128)(2,1)} %collective-permute-done.refs_0_.refs_1_), channel_id=1, source_target_pairs={{0,4},{4,0},{8,12},{12,8},{16,20},{20,16},{24,28},{28,24},{32,36},... | collective-permute-start | bytes 3145736 | tf_op jit(solution)/shard_map/ppermute | solution.py:266
  84.7 26.7 %copy-start.17 = (bf16[256,1024]{1,0:T(8,128)(2,1)}, bf16[256,1024]{1,0:T(8,128)(2,1)S(1)}, u32[]{:S(2)}) copy-start(bf16[256,1024]{1,0:T(8,128)(2,1)S(1)} %collective-permute-done.13.refs_8_) | copy-start | bytes 1572868
  84.7 26.7 %collective-permute-start.5 = (bf16[512,1024]{1,0:T(8,128)(2,1)S(1)}, bf16[512,1024]{1,0:T(8,128)(2,1)S(1)}, u32[]{:S(2)}, u32[]{:S(2)}) collective-permute-start(bf16[512,1024]{1,0:T(8,128)(2,1)S(1)} %shard_map.115.refs_0_.refs_10_), channel_id=1, source_target_pairs={{0,4},{4,0},{8,12},{12,8},{16,20},{20,16},{24,28},{28,24},{32,36},... | collective-permute-start | bytes 3145736 | tf_op jit(solution)/shard_map/ppermute | solution.py:266
  100.0 11.5 %copy-start.6 = (bf16[512,1024]{1,0:T(8,128)(2,1)}, bf16[512,1024]{1,0:T(8,128)(2,1)S(1)}, u32[]{:S(2)}) copy-start(bf16[512,1024]{1,0:T(8,128)(2,1)S(1)} %collective-permute-done.3.refs_1_.refs_2_.refs_12_) | copy-start | bytes 3145732
  100.0 11.4 %collective-permute-start.7 = (bf16[512,1024]{1,0:T(8,128)(2,1)S(1)}, bf16[512,1024]{1,0:T(8,128)(2,1)S(1)}, u32[]{:S(2)}, u32[]{:S(2)}) collective-permute-start(bf16[512,1024]{1,0:T(8,128)(2,1)S(1)} %collective-permute-done.3.refs_1_.refs_2_.refs_12_), channel_id=1, source_target_pairs={{0,4},{4,0},{8,12},{12,8},{16,20},{20,16},{24,28},{28,24},{32,36},... | collective-permute-start | bytes 3145736 | tf_op jit(solution)/shard_map/ppermute | solution.py:266
  100.0 11.5 %copy-start.7 = (bf16[512,1024]{1,0:T(8,128)(2,1)}, bf16[512,1024]{1,0:T(8,128)(2,1)S(1)}, u32[]{:S(2)}) copy-start(bf16[512,1024]{1,0:T(8,128)(2,1)S(1)} %collective-permute-done.2.refs_0_.refs_1_.refs_11_) | copy-start | bytes 3145732
  100.0 11.4 %collective-permute-start.6 = (bf16[512,1024]{1,0:T(8,128)(2,1)S(1)}, bf16[512,1024]{1,0:T(8,128)(2,1)S(1)}, u32[]{:S(2)}, u32[]{:S(2)}) collective-permute-start(bf16[512,1024]{1,0:T(8,128)(2,1)S(1)} %collective-permute-done.2.refs_0_.refs_1_.refs_11_), channel_id=1, source_target_pairs={{0,4},{4,0},{8,12},{12,8},{16,20},{20,16},{24,28},{28,24},{32,36},... | collective-permute-start | bytes 3145736 | tf_op jit(solution)/shard_map/ppermute | solution.py:266
  101.1 10.2 %copy-start.11 = (bf16[512,1024]{1,0:T(8,128)(2,1)}, bf16[512,1024]{1,0:T(8,128)(2,1)S(1)}, u32[]{:S(2)}) copy-start(bf16[512,1024]{1,0:T(8,128)(2,1)S(1)} %collective-permute-done.12.refs_7_) | copy-start | bytes 3145732
  101.1 14.8 %collective-permute-start.4 = (bf16[256,1024]{1,0:T(8,128)(2,1)S(1)}, bf16[256,1024]{1,0:T(8,128)(2,1)S(1)}, u32[]{:S(2)}, u32[]{:S(2)}) collective-permute-start(bf16[256,1024]{1,0:T(8,128)(2,1)S(1)} %get-tuple-element.34), channel_id=1, source_target_pairs={{0,1},{1,2},{2,3},{3,0},{4,5},{5,6},{6,7},{7,4},{8,9},{9,10},{10,1... | collective-permute-start | bytes 1572872 | tf_op jit(solution)/shard_map/ppermute | solution.py:260
  104.1 7.3 %copy-start.12 = (bf16[512,1024]{1,0:T(8,128)(2,1)}, bf16[512,1024]{1,0:T(8,128)(2,1)S(1)}, u32[]{:S(2)}) copy-start(bf16[512,1024]{1,0:T(8,128)(2,1)S(1)} %collective-permute-done.11.refs_6_) | copy-start | bytes 3145732
  104.1 15.3 %collective-permute-start.15 = (bf16[256,1024]{1,0:T(8,128)(2,1)S(1)}, bf16[256,1024]{1,0:T(8,128)(2,1)S(1)}, u32[]{:S(2)}, u32[]{:S(2)}) collective-permute-start(bf16[256,1024]{1,0:T(8,128)(2,1)S(1)} %get-tuple-element.37), channel_id=1, source_target_pairs={{0,3},{1,0},{2,1},{3,2},{4,7},{5,4},{6,5},{7,6},{8,11},{9,8},{10,9... | collective-permute-start | bytes 1572872 | tf_op jit(solution)/shard_map/ppermute | solution.py:263
  104.1 7.3 %copy-start.5 = (bf16[1,192,4096]{2,1,0:T(8,128)(2,1)S(1)}, bf16[1,192,4096]{2,1,0:T(8,128)(2,1)}, u32[]{:S(2)}) copy-start(bf16[1,192,4096]{2,1,0:T(8,128)(2,1)} %param.14) | copy-start | bytes 4718596
  116.0 7.0 %copy-start.9 = (bf16[256,1024]{1,0:T(8,128)(2,1)}, bf16[256,1024]{1,0:T(8,128)(2,1)S(1)}, u32[]{:S(2)}) copy-start(bf16[256,1024]{1,0:T(8,128)(2,1)S(1)} %shard_map.119.refs_0_.refs_13_) | copy-start | bytes 1572868
  116.0 3.4 %collective-permute-start.16 = (bf16[256,1024]{1,0:T(8,128)(2,1)S(1)}, bf16[256,1024]{1,0:T(8,128)(2,1)S(1)}, u32[]{:S(2)}, u32[]{:S(2)}) collective-permute-start(bf16[256,1024]{1,0:T(8,128)(2,1)S(1)} %shard_map.119.refs_0_.refs_13_), channel_id=1, source_target_pairs={{0,4},{4,0},{8,12},{12,8},{16,20},{20,16},{24,28},{28,24},{32,36},... | collective-permute-start | bytes 1572872 | tf_op jit(solution)/shard_map/ppermute | solution.py:266
  119.4 1.9 collective-permute-start.17
  123.0 9.9 %copy-start.4 = (bf16[1024,384]{1,0:T(8,128)(2,1)}, bf16[1024,384]{1,0:T(8,128)(2,1)S(1)}, u32[]{:S(2)}) copy-start(bf16[1024,384]{1,0:T(8,128)(2,1)S(1)} %get-tuple-element.39.refs_0_.refs_21_) | copy-start | bytes 2359300
  124.9 3.7 %collective-permute-start.18 = (bf16[512,1024]{1,0:T(8,128)(2,1)S(1)}, bf16[512,1024]{1,0:T(8,128)(2,1)S(1)}, u32[]{:S(2)}, u32[]{:S(2)}) collective-permute-start(bf16[512,1024]{1,0:T(8,128)(2,1)S(1)} %get-tuple-element.41), channel_id=1, source_target_pairs={{0,4},{4,0},{8,12},{12,8},{16,20},{20,16},{24,28},{28,24},{32,36},... | collective-permute-start | bytes 3145736 | tf_op jit(solution)/shard_map/ppermute | solution.py:266
  128.0 6.8 %collective-permute-start.20 = (bf16[512,1024]{1,0:T(8,128)(2,1)S(1)}, bf16[512,1024]{1,0:T(8,128)(2,1)S(1)}, u32[]{:S(2)}, u32[]{:S(2)}) collective-permute-start(bf16[512,1024]{1,0:T(8,128)(2,1)S(1)} %get-tuple-element.46), channel_id=1, source_target_pairs={{0,4},{4,0},{8,12},{12,8},{16,20},{20,16},{24,28},{28,24},{32,36},... | collective-permute-start | bytes 3145736 | tf_op jit(solution)/shard_map/ppermute | solution.py:266
  128.4 6.4 %collective-permute-start.22 = (bf16[512,1024]{1,0:T(8,128)(2,1)S(1)}, bf16[512,1024]{1,0:T(8,128)(2,1)S(1)}, u32[]{:S(2)}, u32[]{:S(2)}) collective-permute-start(bf16[512,1024]{1,0:T(8,128)(2,1)S(1)} %get-tuple-element.48), channel_id=1, source_target_pairs={{0,4},{4,0},{8,12},{12,8},{16,20},{20,16},{24,28},{28,24},{32,36},... | collective-permute-start | bytes 3145736 | tf_op jit(solution)/shard_map/ppermute | solution.py:266
  129.4 15.7 %collective-permute-start.23 = (bf16[256,1024]{1,0:T(8,128)(2,1)S(1)}, bf16[256,1024]{1,0:T(8,128)(2,1)S(1)}, u32[]{:S(2)}, u32[]{:S(2)}) collective-permute-start(bf16[256,1024]{1,0:T(8,128)(2,1)S(1)} %get-tuple-element.49), channel_id=1, source_target_pairs={{0,3},{1,0},{2,1},{3,2},{4,7},{5,4},{6,5},{7,6},{8,11},{9,8},{10,9... | collective-permute-start | bytes 1572872 | tf_op jit(solution)/shard_map/ppermute | solution.py:263
  129.7 15.4 %collective-permute-start.21 = (bf16[256,1024]{1,0:T(8,128)(2,1)S(1)}, bf16[256,1024]{1,0:T(8,128)(2,1)S(1)}, u32[]{:S(2)}, u32[]{:S(2)}) collective-permute-start(bf16[256,1024]{1,0:T(8,128)(2,1)S(1)} %get-tuple-element.43.refs_3_), channel_id=1, source_target_pairs={{0,1},{1,2},{2,3},{3,0},{4,5},{5,6},{6,7},{7,4},{8,9},{9,10},{10,1... | collective-permute-start | bytes 1572872 | tf_op jit(solution)/shard_map/ppermute | solution.py:260
  134.7 18.5 %collective-permute-start.19 = (bf16[512,1024]{1,0:T(8,128)(2,1)S(1)}, bf16[512,1024]{1,0:T(8,128)(2,1)S(1)}, u32[]{:S(2)}, u32[]{:S(2)}) collective-permute-start(bf16[512,1024]{1,0:T(8,128)(2,1)S(1)} %get-tuple-element.45), channel_id=1, source_target_pairs={{0,4},{4,0},{8,12},{12,8},{16,20},{20,16},{24,28},{28,24},{32,36},... | collective-permute-start | bytes 3145736 | tf_op jit(solution)/shard_map/ppermute | solution.py:266
  147.0 15.3 %collective-permute-start.24 = (bf16[512,512]{1,0:T(8,128)(2,1)S(1)}, bf16[512,512]{1,0:T(8,128)(2,1)S(1)}, u32[]{:S(2)}, u32[]{:S(2)}) collective-permute-start(bf16[512,512]{1,0:T(8,128)(2,1)S(1)} %get-tuple-element.50), channel_id=1, source_target_pairs={{0,1},{1,2},{2,3},{3,0},{4,5},{5,6},{6,7},{7,4},{8,9},{9,10},{10,1... | collective-permute-start | bytes 1572872 | tf_op jit(solution)/shard_map/ppermute | solution.py:260
  149.9 16.1 %collective-permute-start.25 = (bf16[512,512]{1,0:T(8,128)(2,1)S(1)}, bf16[512,512]{1,0:T(8,128)(2,1)S(1)}, u32[]{:S(2)}, u32[]{:S(2)}) collective-permute-start(bf16[512,512]{1,0:T(8,128)(2,1)S(1)} %get-tuple-element.51), channel_id=1, source_target_pairs={{0,3},{1,0},{2,1},{3,2},{4,7},{5,4},{6,5},{7,6},{8,11},{9,8},{10,9... | collective-permute-start | bytes 1572872 | tf_op jit(solution)/shard_map/ppermute | solution.py:263
  149.9 31.6 %collective-permute-start.26 = (bf16[512,512]{1,0:T(8,128)(2,1)}, bf16[512,512]{1,0:T(8,128)(2,1)}, u32[]{:S(2)}, u32[]{:S(2)}) collective-permute-start(bf16[512,512]{1,0:T(8,128)(2,1)} %get-tuple-element.52), channel_id=1, source_target_pairs={{0,1},{1,2},{2,3},{3,0},{4,5},{5,6},{6,7},{7,4},{8,9},{9,10},{10,1... | collective-permute-start | bytes 1572872 | tf_op jit(solution)/shard_map/ppermute | solution.py:260
  153.2 28.4 %collective-permute-start.27 = (bf16[512,512]{1,0:T(8,128)(2,1)}, bf16[512,512]{1,0:T(8,128)(2,1)}, u32[]{:S(2)}, u32[]{:S(2)}) collective-permute-start(bf16[512,512]{1,0:T(8,128)(2,1)} %get-tuple-element.53), channel_id=1, source_target_pairs={{0,3},{1,0},{2,1},{3,2},{4,7},{5,4},{6,5},{7,6},{8,11},{9,8},{10,9... | collective-permute-start | bytes 1572872 | tf_op jit(solution)/shard_map/ppermute | solution.py:263
  167.6 26.4 %all-to-all-start.2 = ((bf16[32,16,512]{2,1,0:T(8,128)(2,1)}), bf16[32,16,512]{2,1,0:T(8,128)(2,1)}, u32[]{:S(2)}, u32[]{:S(2)}) async-start(bf16[32,16,512]{2,1,0:T(8,128)(2,1)} %bitcast.9), calls=%async_computation.2 | async-start | bytes 1048576 | tf_op jit(solution)/shard_map/all_to_all | solution.py:271
  194.0 20.8 %all-to-all-start.3 = ((bf16[32,16,512]{2,1,0:T(8,128)(2,1)}), bf16[32,16,512]{2,1,0:T(8,128)(2,1)}, u32[]{:S(2)}, u32[]{:S(2)}) async-start(bf16[32,16,512]{2,1,0:T(8,128)(2,1)} %bitcast.11), calls=%async_computation.3 | async-start | bytes 1048576 | tf_op jit(solution)/shard_map/all_to_all | solution.py:271
  (7 other events, 18.1 us)

commit v3 on v2

--- a/solution.py
+++ b/solution.py
@@ -66,11 +66,10 @@
     out_ref[...] = scaled.astype(BF16)
 
 
-def combine(masks_ref, *refs):
-    out_ref = refs[-1]
-    half = refs[0].shape[1]
-    for i, back_ref in enumerate(refs[:-1]):
-        out_ref[:, i * half : (i + 1) * half] = dot(masks_ref[...], back_ref[...]).astype(BF16)
+def combine(masks_ref, first_ref, second_ref, out_ref):
+    cut = second_ref.shape[1]
+    out_ref[:, cut:] = dot(masks_ref[...], first_ref[...]).astype(BF16)
+    out_ref[:, :cut] = dot(masks_ref[...], second_ref[...]).astype(BF16)
 
 
 def columns(near_ref, place, width):
@@ -148,8 +147,8 @@
 
 def add_beside(near_ref, a_ref, b_ref, lo_ref, c_ref, d_ref, hi_ref, *outs):
     h, part = lo_ref.shape
-    for i in range(2):
-        cols = slice(i * part // 2, (i + 1) * part // 2)
+    border = outs[1].shape[1]
+    for i, cols in enumerate((slice(border, part), slice(0, border))):
         for a, b, extra, at, out in ((a_ref, b_ref, lo_ref, 0, outs[i]), (c_ref, d_ref, hi_ref, 1, outs[2 + i])):
             for side in range(2):
                 here = slice(side * h, (side + 1) * h)
@@ -211,9 +210,8 @@
         if place is None:
             return pl.BlockSpec(a.shape, lambda i, s: (0,) * len(a.shape), pipeline_mode=one)
         if isinstance(place, str):
-            return pl.BlockSpec(
-                (a.shape[0], a.shape[1] // 2), lambda i, s: (0, int(place)), pipeline_mode=one
-            )
+            at, wide = map(int, place.split())
+            return pl.BlockSpec((a.shape[0], wide), lambda i, s: (0, at), pipeline_mode=one)
         if isinstance(place, tuple):
             return pl.BlockSpec(
                 (a.shape[0] // place[1], a.shape[1]), lambda i, s: (place[0], 0), pipeline_mode=one
@@ -325,7 +323,9 @@
         specs=[None] * 4 + [3] + [None] * 3,
     )
 
-    side = like((rows, part // 2), BF16)
+    narrow = part // 4
+    sides = [like((rows, narrow), BF16), like((rows, part - narrow), BF16)]
+    halves = [f"3 {narrow}", f"0 {part - narrow}"]
     far = call(term_block, near, (both, wg, wu), [block] * 2, specs=[None, 3, 3])
     beside = call(
         near_blocks, near, (both, *(wg, wu) * 2), [block] * 4, specs=[None, 2, 2, 1, 1], deps=far[:1]
@@ -336,13 +336,13 @@
         add_beside,
         near,
         (beside[0], swap(beside[1]), right(lo), beside[2], swap(beside[3]), left(hi)),
-        [side] * 4,
+        sides * 2,
     )
     own = (own[0], swap(own[1]))
 
     def total(i, deps=()):
         args = (*own, right(sums[i]), left(sums[2 + i]))
-        return call(add_last, near, args, [side], specs=[str(i)] * 2 + [None] * 2, deps=deps, flops=10**12)[0]
+        return call(add_last, near, args, sides[i : i + 1], specs=[halves[i]] * 2 + [None] * 2, deps=deps, flops=10**12)[0]
 
     first = total(0)
     back = [exchange(first), exchange(total(1, (first,)))]

time: 218 us -> 219 us (level); the launches traced: 217 us -> 216 us
  waiting for transfers between devices: 101 us -> 98.1 us
    ppermute x7, waiting for transfers between devices: 11.2 us -> 5.62 us  [right(): return lax.ppermute(a, 'dp', turn)]
  transfers between devices with their start and end apart: 32 -> 32, of which waited for: 13 -> 14; matrix products, arithmetic and copies ran while one was open for 0% -> 0% of each run, Pallas kernels for 19% -> 20%
where the time goes in v3:
time: 219 us; the launch traced here: 216 us
  waiting for transfers between devices  98.1 us (45%)
  starting transfers between devices  65.4 us (30%)
  Pallas kernels  51 us (23%)
    ppermute x7, waiting for transfers between devices, left(): return lax.ppermute(a, 'dp', back_turn)  46.3 us
    pallas_call x13, Pallas kernels, call(): pl.pallas_call(body, grid_spec=pltpu.PrefetchScalarGridSpec(num_scalar_pr...  42.3 us
    all_to_all x4, waiting for transfers between devices, exchange(): lax.all_to_all(a, 'expert', split_axis=0, concat_axis=0, tiled=True, axis...  41.4 us
    all_to_all x4, starting transfers between devices, exchange(): lax.all_to_all(a, 'expert', split_axis=0, concat_axis=0, tiled=True, axis...  40.5 us
    ppermute x7, starting transfers between devices, right(): return lax.ppermute(a, 'dp', turn)  21.3 us
    pallas_call x2, Pallas kernels, slots(): pl.pallas_call(functools.partial(kernel, experts, capacity), in_specs=[vm...  6.44 us
    ppermute x7, waiting for transfers between devices, right(): return lax.ppermute(a, 'dp', turn)  5.62 us
    ppermute x14, waiting for transfers between devices, swap(): return lax.ppermute(a, 'expert', swap_pairs)  4.79 us
  transfers between devices with their start and end apart: 32, of which 14 were waited for; matrix products, arithmetic and copies ran while one was open for 0% of the time, Pallas kernels for 20%

profile of v3, /device:TPU:30, one launch (start us, length us, event | category | flops | bytes accessed | tf_op | source)
XLA Modules:
  0.0 215.7 jit_solution(765230301286557497)
XLA Ops:
  0.6 3.0 %shard_map.112 = bf16[512,1024]{1,0:T(8,128)(2,1)} custom-call(s32[2,128]{1,0:T(2,128)} %bitcast.31, bf16[128,4096]{1,0:T(8,128)(2,1)} %tok_ref.1), custom_call_target="tpu_custom_call" | custom-call | tf_op jit(solution)/shard_map/pallas_call | solution.py:284
  3.7 11.6 %all-to-all-start.1 = ((bf16[32,16,1024]{2,1,0:T(8,128)(2,1)}), bf16[32,16,1024]{2,1,0:T(8,128)(2,1)S(1)}, u32[]{:S(2)}, u32[]{:S(2)}) async-start(bf16[32,16,1024]{2,1,0:T(8,128)(2,1)} %bitcast.30), calls=%async_computation.1 | async-start | bytes 2097152 | tf_op jit(solution)/shard_map/all_to_all | solution.py:269
  15.3 3.4 %shard_map.111 = (bf16[512,1024]{1,0:T(8,128)(2,1)}, bf16[128,512]{1,0:T(8,128)(2,1)}) custom-call(s32[2,128]{1,0:T(2,128)} %bitcast.32, f32[2,128]{1,0:T(2,128)} %bitcast.33, bf16[128,4096]{1,0:T(8,128)(2,1)} %cot_ref.1), custom_call_target="tpu_custom_call" | custom-call | tf_op jit(solution)/shard_map/pallas_call | solution.py:284
  18.7 23.0 %all-to-all-done.1 = bf16[32,16,1024]{2,1,0:T(8,128)(2,1)S(1)} async-done(((bf16[32,16,1024]{2,1,0:T(8,128)(2,1)}), bf16[32,16,1024]{2,1,0:T(8,128)(2,1)S(1)}, u32[]{:S(2)}, u32[]{:S(2)}) %all-to-all-start.1) | async-done | bytes 1048608 | tf_op jit(solution)/shard_map/all_to_all | solution.py:269
  41.7 0.7 collective-permute-start.1
  42.4 2.5 %collective-permute-start = (bf16[512,1024]{1,0:T(8,128)(2,1)S(1)}, bf16[512,1024]{1,0:T(8,128)(2,1)}, u32[]{:S(2)}, u32[]{:S(2)}) collective-permute-start(bf16[512,1024]{1,0:T(8,128)(2,1)S(1)} %shard_map.113.refs_0_), channel_id=1, source_target_pairs={{0,1},{1,2},{2,3},{3,0},{4,5},{5,6},{6,7},{7,4},{8,9},{9,10},{10,1... | collective-permute-start | bytes 3145736 | tf_op jit(solution)/shard_map/ppermute | solution.py:258
  44.9 7.3 %all-to-all-start = ((bf16[32,16,1024]{2,1,0:T(8,128)(2,1)}), bf16[32,16,1024]{2,1,0:T(8,128)(2,1)S(1)}, u32[]{:S(2)}, u32[]{:S(2)}) async-start(bf16[32,16,1024]{2,1,0:T(8,128)(2,1)} %bitcast.2), calls=%async_computation | async-start | bytes 2097152 | tf_op jit(solution)/shard_map/all_to_all | solution.py:269
  52.4 11.9 %collective-permute-done.1.refs_1_.refs_2_ = bf16[512,1024]{1,0:T(8,128)(2,1)S(1)} collective-permute-done((bf16[512,1024]{1,0:T(8,128)(2,1)S(1)}, bf16[512,1024]{1,0:T(8,128)(2,1)S(1)}, u32[]{:S(2)}, u32[]{:S(2)}) %collective-permute-start.1) | collective-permute-done | bytes 1048608 | tf_op jit(solution)/shard_map/ppermute | solution.py:261
  64.3 2.6 %shard_map.114 = (bf16[256,1024]{1,0:T(8,128)(2,1)}, bf16[256,1024]{1,0:T(8,128)(2,1)}) custom-call(s32[4]{0:T(128)S(1)} %and_select_fusion.near_ref, bf16[512,1024]{1,0:T(8,128)(2,1)} %collective-permute-done.refs_0_.refs_1_, bf16[512,1024]{1,0:T(8,128)(2,1)S(1)} %collective-permute-done.1.refs_1_.refs_2_), custom_call_target="tpu_custom_call" | custom-call | flops 49999998976 | tf_op jit(solution)/shard_map/pallas_call | solution.py:228
  66.9 3.2 %collective-permute-start.8 = (bf16[256,1024]{1,0:T(8,128)(2,1)}, bf16[256,1024]{1,0:T(8,128)(2,1)}, u32[]{:S(2)}, u32[]{:S(2)}) collective-permute-start(bf16[256,1024]{1,0:T(8,128)(2,1)} %get-tuple-element.33.refs_1_), channel_id=1, source_target_pairs={{0,1},{1,2},{2,3},{3,0},{4,5},{5,6},{6,7},{7,4},{8,9},{9,10},{10,1... | collective-permute-start | bytes 1572872 | tf_op jit(solution)/shard_map/ppermute | solution.py:258
  70.1 7.6 %all-to-all-done = bf16[32,16,1024]{2,1,0:T(8,128)(2,1)S(1)} async-done(((bf16[32,16,1024]{2,1,0:T(8,128)(2,1)}), bf16[32,16,1024]{2,1,0:T(8,128)(2,1)S(1)}, u32[]{:S(2)}, u32[]{:S(2)}) %all-to-all-start) | async-done | bytes 1048608 | tf_op jit(solution)/shard_map/all_to_all | solution.py:269
  77.8 3.2 %collective-permute-start.2 = (bf16[512,1024]{1,0:T(8,128)(2,1)S(1)}, bf16[512,1024]{1,0:T(8,128)(2,1)S(1)}, u32[]{:S(2)}, u32[]{:S(2)}) collective-permute-start(bf16[512,1024]{1,0:T(8,128)(2,1)S(1)} %shard_map.115.refs_0_.refs_10_), channel_id=1, source_target_pairs={{0,1},{1,2},{2,3},{3,0},{4,5},{5,6},{6,7},{7,4},{8,9},{9,10},{10,1... | collective-permute-start | bytes 3145736 | tf_op jit(solution)/shard_map/ppermute | solution.py:258
  81.1 0.5 collective-permute-start.13
  81.7 1.5 collective-permute-done.14.refs_9_
  83.3 1.4 collective-permute-done.13.refs_8_
  84.8 15.2 %collective-permute-done.3.refs_1_.refs_2_.refs_12_ = bf16[512,1024]{1,0:T(8,128)(2,1)S(1)} collective-permute-done((bf16[512,1024]{1,0:T(8,128)(2,1)S(1)}, bf16[512,1024]{1,0:T(8,128)(2,1)S(1)}, u32[]{:S(2)}, u32[]{:S(2)}) %collective-permute-start.3) | collective-permute-done | bytes 1048608 | tf_op jit(solution)/shard_map/ppermute | solution.py:261
  100.0 0.5 collective-permute-start.6
  100.5 0.6 shard_map.116
  101.1 3.0 %collective-permute-start.4 = (bf16[256,1024]{1,0:T(8,128)(2,1)S(1)}, bf16[256,1024]{1,0:T(8,128)(2,1)S(1)}, u32[]{:S(2)}, u32[]{:S(2)}) collective-permute-start(bf16[256,1024]{1,0:T(8,128)(2,1)S(1)} %get-tuple-element.34), channel_id=1, source_target_pairs={{0,1},{1,2},{2,3},{3,0},{4,5},{5,6},{6,7},{7,4},{8,9},{9,10},{10,1... | collective-permute-start | bytes 1572872 | tf_op jit(solution)/shard_map/ppermute | solution.py:258
  104.2 7.2 %shard_map.117 = (f32[1024,192]{1,0:T(8,128)S(1)}, f32[1024,192]{1,0:T(8,128)S(1)}) custom-call(s32[4]{0:T(128)S(1)} %and_select_fusion.near_ref, bf16[512,1024]{1,0:T(8,128)(2,1)S(1)} %shard_map.113.refs_0_, bf16[512,1024]{1,0:T(8,128)(2,1)} %collective-permute-done.refs_0_.refs_1_, bf16[512,1024]{1,0:T(8,128)(2,1)S(1)} %collective-permute-done.1.refs_1_.refs_2_, ...), custom_call_target="tpu_custom_call" | custom-call | tf_op jit(solution)/shard_map/pallas_call | solution.py:228
  111.5 2.3 %shard_map.118.refs_1_.refs_7_ = f32[1024,192]{1,0:T(8,128)S(1)} custom-call(s32[4]{0:T(128)S(1)} %and_select_fusion.near_ref, bf16[512,1024]{1,0:T(8,128)(2,1)S(1)} %shard_map.115.refs_0_.refs_10_, bf16[512,1024]{1,0:T(8,128)(2,1)S(1)} %collective-permute-done.2.refs_0_.refs_1_.refs_11_, ...), custom_call_target="tpu_custom_call" | custom-call | tf_op jit(solution)/shard_map/pallas_call | solution.py:228
  113.9 2.1 collective-permute-done.4.refs_0_
  116.0 3.4 %collective-permute-done.15.refs_0_ = bf16[256,1024]{1,0:T(8,128)(2,1)S(1)} collective-permute-done((bf16[256,1024]{1,0:T(8,128)(2,1)S(1)}, bf16[256,1024]{1,0:T(8,128)(2,1)S(1)}, u32[]{:S(2)}, u32[]{:S(2)}) %collective-permute-start.15) | collective-permute-done | bytes 524320 | tf_op jit(solution)/shard_map/ppermute | solution.py:261
  119.4 1.9 collective-permute-done.17.refs_3_.refs_19_
  121.3 1.7 shard_map.121
  123.0 1.8 shard_map.122
  124.9 0.2 collective-permute-start.18
  125.1 2.9 %shard_map.123 = (bf16[512,1024]{1,0:T(8,128)(2,1)S(1)}, bf16[512,1024]{1,0:T(8,128)(2,1)S(1)}, bf16[512,1024]{1,0:T(8,128)(2,1)S(1)}, bf16[512,1024]{1,0:T(8,128)(2,1)S(1)}) custom-call(s32[4]{0:T(128)S(1)} %and_select_fusion.near_ref, bf16[1024,384]{1,0:T(8,128)(2,1)S(1)} %get-tuple-element.39.refs_0_.refs_21_, bf16[192,4096]{1,0:T(8,128)(2,1)S(1)} %bitcast.18, ...), custom_call_target="tpu_custom_call" | custom-call | tf_op jit(solution)/shard_map/pallas_call | solution.py:228
  128.0 0.5 collective-permute-start.20
  128.4 0.3 collective-permute-start.22
  128.8 0.8 shard_map.124
  129.5 1.8 shard_map.125
  131.3 0.3 collective-permute-start.19
  131.6 3.2 %collective-permute-start.21 = (bf16[256,1024]{1,0:T(8,128)(2,1)S(1)}, bf16[256,1024]{1,0:T(8,128)(2,1)S(1)}, u32[]{:S(2)}, u32[]{:S(2)}) collective-permute-start(bf16[256,1024]{1,0:T(8,128)(2,1)S(1)} %get-tuple-element.43.refs_3_), channel_id=1, source_target_pairs={{0,1},{1,2},{2,3},{3,0},{4,5},{5,6},{6,7},{7,4},{8,9},{9,10},{10,1... | collective-permute-start | bytes 1572872 | tf_op jit(solution)/shard_map/ppermute | solution.py:258
  134.9 12.1 %collective-permute-done.23.refs_5_ = bf16[256,1024]{1,0:T(8,128)(2,1)S(1)} collective-permute-done((bf16[256,1024]{1,0:T(8,128)(2,1)S(1)}, bf16[256,1024]{1,0:T(8,128)(2,1)S(1)}, u32[]{:S(2)}, u32[]{:S(2)}) %collective-permute-start.23) | collective-permute-done | bytes 524320 | tf_op jit(solution)/shard_map/ppermute | solution.py:261
  147.0 2.0 shard_map.126
  149.0 3.0 %collective-permute-start.24 = (bf16[512,256]{1,0:T(8,128)(2,1)S(1)}, bf16[512,256]{1,0:T(8,128)(2,1)S(1)}, u32[]{:S(2)}, u32[]{:S(2)}) collective-permute-start(bf16[512,256]{1,0:T(8,128)(2,1)S(1)} %get-tuple-element.50), channel_id=1, source_target_pairs={{0,1},{1,2},{2,3},{3,0},{4,5},{5,6},{6,7},{7,4},{8,9},{9,10},{10,1... | collective-permute-start | bytes 786440 | tf_op jit(solution)/shard_map/ppermute | solution.py:258
  151.9 3.2 %collective-permute-start.26 = (bf16[512,768]{1,0:T(8,128)(2,1)}, bf16[512,768]{1,0:T(8,128)(2,1)}, u32[]{:S(2)}, u32[]{:S(2)}) collective-permute-start(bf16[512,768]{1,0:T(8,128)(2,1)} %get-tuple-element.52), channel_id=1, source_target_pairs={{0,1},{1,2},{2,3},{3,0},{4,5},{5,6},{6,7},{7,4},{8,9},{9,10},{10,1... | collective-permute-start | bytes 2359304 | tf_op jit(solution)/shard_map/ppermute | solution.py:258
  155.2 3.5 %collective-permute-done.24.refs_2_ = bf16[512,256]{1,0:T(8,128)(2,1)S(1)} collective-permute-done((bf16[512,256]{1,0:T(8,128)(2,1)S(1)}, bf16[512,256]{1,0:T(8,128)(2,1)S(1)}, u32[]{:S(2)}, u32[]{:S(2)}) %collective-permute-start.24) | collective-permute-done | bytes 262176 | tf_op jit(solution)/shard_map/ppermute | solution.py:258
  158.7 3.7 %collective-permute-done.25.refs_3_ = bf16[512,256]{1,0:T(8,128)(2,1)S(1)} collective-permute-done((bf16[512,256]{1,0:T(8,128)(2,1)S(1)}, bf16[512,256]{1,0:T(8,128)(2,1)S(1)}, u32[]{:S(2)}, u32[]{:S(2)}) %collective-permute-start.25) | collective-permute-done | bytes 262176 | tf_op jit(solution)/shard_map/ppermute | solution.py:261
  162.4 1.4 shard_map.127.refs_4_
  163.8 13.9 %all-to-all-start.2 = ((bf16[32,16,256]{2,1,0:T(8,128)(2,1)}), bf16[32,16,256]{2,1,0:T(8,128)(2,1)}, u32[]{:S(2)}, u32[]{:S(2)}) async-start(bf16[32,16,256]{2,1,0:T(8,128)(2,1)} %bitcast.9), calls=%async_computation.2 | async-start | bytes 524288 | tf_op jit(solution)/shard_map/all_to_all | solution.py:269
  177.7 3.3 %shard_map.128 = bf16[512,768]{1,0:T(8,128)(2,1)} custom-call(s32[4]{0:T(128)S(1)} %and_select_fusion.near_ref, bf16[512,1024]{1,0:T(8,128)(2,1)S(1)} %get-tuple-element.44.refs_0_, bf16[512,1024]{1,0:T(8,128)(2,1)S(1)} %collective-permute-done.19.refs_1_, bf16[512,768]{1,0:T(8,128)(2,1)} %collective-permute-done.26.refs_2_, ...), custom_call_target="tpu_custom_call" | custom-call | flops 999999995904 | tf_op jit(solution)/shard_map/pallas_call | solution.py:228
  181.0 5.8 %all-to-all-done.2 = bf16[32,16,256]{2,1,0:T(8,128)(2,1)} async-done(((bf16[32,16,256]{2,1,0:T(8,128)(2,1)}), bf16[32,16,256]{2,1,0:T(8,128)(2,1)}, u32[]{:S(2)}, u32[]{:S(2)}) %all-to-all-start.2) | async-done | bytes 262176 | tf_op jit(solution)/shard_map/all_to_all | solution.py:269
  186.9 7.6 %all-to-all-start.3 = ((bf16[32,16,768]{2,1,0:T(8,128)(2,1)}), bf16[32,16,768]{2,1,0:T(8,128)(2,1)}, u32[]{:S(2)}, u32[]{:S(2)}) async-start(bf16[32,16,768]{2,1,0:T(8,128)(2,1)} %bitcast.11), calls=%async_computation.3 | async-start | bytes 1572864 | tf_op jit(solution)/shard_map/all_to_all | solution.py:269
  194.5 13.9 %shard_map.130 = (bf16[192,4096]{1,0:T(8,128)(2,1)}, bf16[192,4096]{1,0:T(8,128)(2,1)}, bf16[192,4096]{1,0:T(8,128)(2,1)}) custom-call(s32[4]{0:T(128)} %copy-done.20, bf16[512,1024]{1,0:T(8,128)(2,1)} %copy-done.2, bf16[512,1024]{1,0:T(8,128)(2,1)} %collective-permute-done.refs_0_.refs_1_, bf16[512,1024]{1,0:T(8,128)(2,1)} %copy-done.10, ...), custom_call_target="tpu_custom_call" | custom-call | flops 999999995904 | tf_op jit(solution)/shard_map/pallas_call | solution.py:228
  208.4 5.0 %all-to-all-done.3 = bf16[32,16,768]{2,1,0:T(8,128)(2,1)} async-done(((bf16[32,16,768]{2,1,0:T(8,128)(2,1)}), bf16[32,16,768]{2,1,0:T(8,128)(2,1)}, u32[]{:S(2)}, u32[]{:S(2)}) %all-to-all-start.3) | async-done | bytes 786464 | tf_op jit(solution)/shard_map/all_to_all | solution.py:269
  213.4 2.3 %shard_map.129 = bf16[128,1024]{1,0:T(8,128)(2,1)} custom-call(bf16[128,512]{1,0:T(8,128)(2,1)} %get-tuple-element.31.masks_ref, bf16[512,256]{1,0:T(8,128)(2,1)} %bitcast.10.first_ref, bf16[512,768]{1,0:T(8,128)(2,1)} %bitcast.12.second_ref), custom_call_target="tpu_custom_call" | custom-call | tf_op jit(solution)/shard_map/pallas_call | solution.py:357
  (83 shorter events, 0.7 us)
Async XLA Ops:
  3.7 38.0 %all-to-all-start.1 = ((bf16[32,16,1024]{2,1,0:T(8,128)(2,1)}), bf16[32,16,1024]{2,1,0:T(8,128)(2,1)S(1)}, u32[]{:S(2)}, u32[]{:S(2)}) async-start(bf16[32,16,1024]{2,1,0:T(8,128)(2,1)} %bitcast.30), calls=%async_computation.1 | async-start | bytes 2097152 | tf_op jit(solution)/shard_map/all_to_all | solution.py:269
  41.7 62.4 %copy-start.2 = (bf16[512,1024]{1,0:T(8,128)(2,1)}, bf16[512,1024]{1,0:T(8,128)(2,1)S(1)}, u32[]{:S(2)}) copy-start(bf16[512,1024]{1,0:T(8,128)(2,1)S(1)} %shard_map.113.refs_0_) | copy-start | bytes 3145732
  41.7 10.6 %copy-start.22 = (s32[4]{0:T(128)S(1)}, s32[4]{0:T(128)}, u32[]{:S(2)}) copy-start(s32[4]{0:T(128)} %constant.21.clone) | copy-start | bytes 52
  41.7 22.6 %collective-permute-start.1 = (bf16[512,1024]{1,0:T(8,128)(2,1)S(1)}, bf16[512,1024]{1,0:T(8,128)(2,1)S(1)}, u32[]{:S(2)}, u32[]{:S(2)}) collective-permute-start(bf16[512,1024]{1,0:T(8,128)(2,1)S(1)} %shard_map.113.refs_0_), channel_id=1, source_target_pairs={{0,3},{1,0},{2,1},{3,2},{4,7},{5,4},{6,5},{7,6},{8,11},{9,8},{10,9... | collective-permute-start | bytes 3145736 | tf_op jit(solution)/shard_map/ppermute | solution.py:261
  42.4 21.8 %collective-permute-start = (bf16[512,1024]{1,0:T(8,128)(2,1)S(1)}, bf16[512,1024]{1,0:T(8,128)(2,1)}, u32[]{:S(2)}, u32[]{:S(2)}) collective-permute-start(bf16[512,1024]{1,0:T(8,128)(2,1)S(1)} %shard_map.113.refs_0_), channel_id=1, source_target_pairs={{0,1},{1,2},{2,3},{3,0},{4,5},{5,6},{6,7},{7,4},{8,9},{9,10},{10,1... | collective-permute-start | bytes 3145736 | tf_op jit(solution)/shard_map/ppermute | solution.py:258
  44.9 32.8 %all-to-all-start = ((bf16[32,16,1024]{2,1,0:T(8,128)(2,1)}), bf16[32,16,1024]{2,1,0:T(8,128)(2,1)S(1)}, u32[]{:S(2)}, u32[]{:S(2)}) async-start(bf16[32,16,1024]{2,1,0:T(8,128)(2,1)} %bitcast.2), calls=%async_computation | async-start | bytes 2097152 | tf_op jit(solution)/shard_map/all_to_all | solution.py:269
  52.3 125.4 %copy-start.20 = (s32[4]{0:T(128)}, s32[4]{0:T(128)S(1)}, u32[]{:S(2)}) copy-start(s32[4]{0:T(128)S(1)} %and_select_fusion.near_ref) | copy-start | bytes 52
  52.3 29.3 %collective-permute-start.10 = (bf16[512,1024]{1,0:T(8,128)(2,1)S(1)}, bf16[512,1024]{1,0:T(8,128)(2,1)}, u32[]{:S(2)}, u32[]{:S(2)}) collective-permute-start(bf16[512,1024]{1,0:T(8,128)(2,1)S(1)} %shard_map.113.refs_0_), channel_id=1, source_target_pairs={{0,4},{4,0},{8,12},{12,8},{16,20},{20,16},{24,28},{28,24},{32,36},... | collective-permute-start | bytes 3145736 | tf_op jit(solution)/shard_map/ppermute | solution.py:264
  64.3 39.9 %copy-start.10 = (bf16[512,1024]{1,0:T(8,128)(2,1)}, bf16[512,1024]{1,0:T(8,128)(2,1)S(1)}, u32[]{:S(2)}) copy-start(bf16[512,1024]{1,0:T(8,128)(2,1)S(1)} %collective-permute-done.1.refs_1_.refs_2_) | copy-start | bytes 3145732
  66.9 14.2 %collective-permute-start.9 = (bf16[256,1024]{1,0:T(8,128)(2,1)}, bf16[256,1024]{1,0:T(8,128)(2,1)}, u32[]{:S(2)}, u32[]{:S(2)}) collective-permute-start(bf16[256,1024]{1,0:T(8,128)(2,1)} %get-tuple-element.35), channel_id=1, source_target_pairs={{0,3},{1,0},{2,1},{3,2},{4,7},{5,4},{6,5},{7,6},{8,11},{9,8},{10,9... | collective-permute-start | bytes 1572872 | tf_op jit(solution)/shard_map/ppermute | solution.py:261
  66.9 14.2 %collective-permute-start.8 = (bf16[256,1024]{1,0:T(8,128)(2,1)}, bf16[256,1024]{1,0:T(8,128)(2,1)}, u32[]{:S(2)}, u32[]{:S(2)}) collective-permute-start(bf16[256,1024]{1,0:T(8,128)(2,1)} %get-tuple-element.33.refs_1_), channel_id=1, source_target_pairs={{0,1},{1,2},{2,3},{3,0},{4,5},{5,6},{6,7},{7,4},{8,9},{9,10},{10,1... | collective-permute-start | bytes 1572872 | tf_op jit(solution)/shard_map/ppermute | solution.py:258
  77.7 26.4 %copy-start.1 = (bf16[1,192,4096]{2,1,0:T(8,128)(2,1)S(1)}, bf16[1,192,4096]{2,1,0:T(8,128)(2,1)}, u32[]{:S(2)}) copy-start(bf16[1,192,4096]{2,1,0:T(8,128)(2,1)} %param.13) | copy-start | bytes 4718596
  77.7 33.7 %copy-start.3 = (bf16[512,1024]{1,0:T(8,128)(2,1)}, bf16[512,1024]{1,0:T(8,128)(2,1)S(1)}, u32[]{:S(2)}) copy-start(bf16[512,1024]{1,0:T(8,128)(2,1)S(1)} %shard_map.115.refs_0_.refs_10_) | copy-start | bytes 3145732
  77.7 26.4 %copy-start = (bf16[1,192,4096]{2,1,0:T(8,128)(2,1)S(1)}, bf16[1,192,4096]{2,1,0:T(8,128)(2,1)}, u32[]{:S(2)}) copy-start(bf16[1,192,4096]{2,1,0:T(8,128)(2,1)} %param.12) | copy-start | bytes 4718596
  77.7 22.2 %collective-permute-start.3 = (bf16[512,1024]{1,0:T(8,128)(2,1)S(1)}, bf16[512,1024]{1,0:T(8,128)(2,1)S(1)}, u32[]{:S(2)}, u32[]{:S(2)}) collective-permute-start(bf16[512,1024]{1,0:T(8,128)(2,1)S(1)} %shard_map.115.refs_0_.refs_10_), channel_id=1, source_target_pairs={{0,3},{1,0},{2,1},{3,2},{4,7},{5,4},{6,5},{7,6},{8,11},{9,8},{10,9... | collective-permute-start | bytes 3145736 | tf_op jit(solution)/shard_map/ppermute | solution.py:261
  77.8 22.2 %collective-permute-start.2 = (bf16[512,1024]{1,0:T(8,128)(2,1)S(1)}, bf16[512,1024]{1,0:T(8,128)(2,1)S(1)}, u32[]{:S(2)}, u32[]{:S(2)}) collective-permute-start(bf16[512,1024]{1,0:T(8,128)(2,1)S(1)} %shard_map.115.refs_0_.refs_10_), channel_id=1, source_target_pairs={{0,1},{1,2},{2,3},{3,0},{4,5},{5,6},{6,7},{7,4},{8,9},{9,10},{10,1... | collective-permute-start | bytes 3145736 | tf_op jit(solution)/shard_map/ppermute | solution.py:258
  81.1 2.1 collective-permute-start.14
  81.1 3.6 %collective-permute-start.13 = (bf16[256,1024]{1,0:T(8,128)(2,1)}, bf16[256,1024]{1,0:T(8,128)(2,1)S(1)}, u32[]{:S(2)}, u32[]{:S(2)}) collective-permute-start(bf16[256,1024]{1,0:T(8,128)(2,1)} %collective-permute-done.8.refs_3_), channel_id=1, source_target_pairs={{0,4},{4,0},{8,12},{12,8},{16,20},{20,16},{24,28},{28,24},{32,36},... | collective-permute-start | bytes 1572872 | tf_op jit(solution)/shard_map/ppermute | solution.py:264
  81.6 19.5 %collective-permute-start.12 = (bf16[512,1024]{1,0:T(8,128)(2,1)S(1)}, bf16[512,1024]{1,0:T(8,128)(2,1)S(1)}, u32[]{:S(2)}, u32[]{:S(2)}) collective-permute-start(bf16[512,1024]{1,0:T(8,128)(2,1)S(1)} %collective-permute-done.1.refs_1_.refs_2_), channel_id=1, source_target_pairs={{0,4},{4,0},{8,12},{12,8},{16,20},{20,16},{24,28},{28,24},{32,36},... | collective-permute-start | bytes 3145736 | tf_op jit(solution)/shard_map/ppermute | solution.py:264
  83.2 28.2 %copy-start.16 = (bf16[256,1024]{1,0:T(8,128)(2,1)}, bf16[256,1024]{1,0:T(8,128)(2,1)S(1)}, u32[]{:S(2)}) copy-start(bf16[256,1024]{1,0:T(8,128)(2,1)S(1)} %collective-permute-done.14.refs_9_) | copy-start | bytes 1572868
  83.2 20.9 %collective-permute-start.11 = (bf16[512,1024]{1,0:T(8,128)(2,1)}, bf16[512,1024]{1,0:T(8,128)(2,1)S(1)}, u32[]{:S(2)}, u32[]{:S(2)}) collective-permute-start(bf16[512,1024]{1,0:T(8,128)(2,1)} %collective-permute-done.refs_0_.refs_1_), channel_id=1, source_target_pairs={{0,4},{4,0},{8,12},{12,8},{16,20},{20,16},{24,28},{28,24},{32,36},... | collective-permute-start | bytes 3145736 | tf_op jit(solution)/shard_map/ppermute | solution.py:264
  84.7 26.7 %copy-start.17 = (bf16[256,1024]{1,0:T(8,128)(2,1)}, bf16[256,1024]{1,0:T(8,128)(2,1)S(1)}, u32[]{:S(2)}) copy-start(bf16[256,1024]{1,0:T(8,128)(2,1)S(1)} %collective-permute-done.13.refs_8_) | copy-start | bytes 1572868
  84.7 26.7 %collective-permute-start.5 = (bf16[512,1024]{1,0:T(8,128)(2,1)S(1)}, bf16[512,1024]{1,0:T(8,128)(2,1)S(1)}, u32[]{:S(2)}, u32[]{:S(2)}) collective-permute-start(bf16[512,1024]{1,0:T(8,128)(2,1)S(1)} %shard_map.115.refs_0_.refs_10_), channel_id=1, source_target_pairs={{0,4},{4,0},{8,12},{12,8},{16,20},{20,16},{24,28},{28,24},{32,36},... | collective-permute-start | bytes 3145736 | tf_op jit(solution)/shard_map/ppermute | solution.py:264
  100.0 11.5 %copy-start.6 = (bf16[512,1024]{1,0:T(8,128)(2,1)}, bf16[512,1024]{1,0:T(8,128)(2,1)S(1)}, u32[]{:S(2)}) copy-start(bf16[512,1024]{1,0:T(8,128)(2,1)S(1)} %collective-permute-done.3.refs_1_.refs_2_.refs_12_) | copy-start | bytes 3145732
  100.0 11.4 %collective-permute-start.7 = (bf16[512,1024]{1,0:T(8,128)(2,1)S(1)}, bf16[512,1024]{1,0:T(8,128)(2,1)S(1)}, u32[]{:S(2)}, u32[]{:S(2)}) collective-permute-start(bf16[512,1024]{1,0:T(8,128)(2,1)S(1)} %collective-permute-done.3.refs_1_.refs_2_.refs_12_), channel_id=1, source_target_pairs={{0,4},{4,0},{8,12},{12,8},{16,20},{20,16},{24,28},{28,24},{32,36},... | collective-permute-start | bytes 3145736 | tf_op jit(solution)/shard_map/ppermute | solution.py:264
  100.0 11.5 %copy-start.7 = (bf16[512,1024]{1,0:T(8,128)(2,1)}, bf16[512,1024]{1,0:T(8,128)(2,1)S(1)}, u32[]{:S(2)}) copy-start(bf16[512,1024]{1,0:T(8,128)(2,1)S(1)} %collective-permute-done.2.refs_0_.refs_1_.refs_11_) | copy-start | bytes 3145732
  100.0 11.4 %collective-permute-start.6 = (bf16[512,1024]{1,0:T(8,128)(2,1)S(1)}, bf16[512,1024]{1,0:T(8,128)(2,1)S(1)}, u32[]{:S(2)}, u32[]{:S(2)}) collective-permute-start(bf16[512,1024]{1,0:T(8,128)(2,1)S(1)} %collective-permute-done.2.refs_0_.refs_1_.refs_11_), channel_id=1, source_target_pairs={{0,4},{4,0},{8,12},{12,8},{16,20},{20,16},{24,28},{28,24},{32,36},... | collective-permute-start | bytes 3145736 | tf_op jit(solution)/shard_map/ppermute | solution.py:264
  101.1 10.2 %copy-start.11 = (bf16[512,1024]{1,0:T(8,128)(2,1)}, bf16[512,1024]{1,0:T(8,128)(2,1)S(1)}, u32[]{:S(2)}) copy-start(bf16[512,1024]{1,0:T(8,128)(2,1)S(1)} %collective-permute-done.12.refs_7_) | copy-start | bytes 3145732
  101.1 14.8 %collective-permute-start.4 = (bf16[256,1024]{1,0:T(8,128)(2,1)S(1)}, bf16[256,1024]{1,0:T(8,128)(2,1)S(1)}, u32[]{:S(2)}, u32[]{:S(2)}) collective-permute-start(bf16[256,1024]{1,0:T(8,128)(2,1)S(1)} %get-tuple-element.34), channel_id=1, source_target_pairs={{0,1},{1,2},{2,3},{3,0},{4,5},{5,6},{6,7},{7,4},{8,9},{9,10},{10,1... | collective-permute-start | bytes 1572872 | tf_op jit(solution)/shard_map/ppermute | solution.py:258
  104.1 7.3 %copy-start.12 = (bf16[512,1024]{1,0:T(8,128)(2,1)}, bf16[512,1024]{1,0:T(8,128)(2,1)S(1)}, u32[]{:S(2)}) copy-start(bf16[512,1024]{1,0:T(8,128)(2,1)S(1)} %collective-permute-done.11.refs_6_) | copy-start | bytes 3145732
  104.1 15.3 %collective-permute-start.15 = (bf16[256,1024]{1,0:T(8,128)(2,1)S(1)}, bf16[256,1024]{1,0:T(8,128)(2,1)S(1)}, u32[]{:S(2)}, u32[]{:S(2)}) collective-permute-start(bf16[256,1024]{1,0:T(8,128)(2,1)S(1)} %get-tuple-element.37), channel_id=1, source_target_pairs={{0,3},{1,0},{2,1},{3,2},{4,7},{5,4},{6,5},{7,6},{8,11},{9,8},{10,9... | collective-permute-start | bytes 1572872 | tf_op jit(solution)/shard_map/ppermute | solution.py:261
  104.1 7.3 %copy-start.5 = (bf16[1,192,4096]{2,1,0:T(8,128)(2,1)S(1)}, bf16[1,192,4096]{2,1,0:T(8,128)(2,1)}, u32[]{:S(2)}) copy-start(bf16[1,192,4096]{2,1,0:T(8,128)(2,1)} %param.14) | copy-start | bytes 4718596
  116.0 7.0 %copy-start.9 = (bf16[256,1024]{1,0:T(8,128)(2,1)}, bf16[256,1024]{1,0:T(8,128)(2,1)S(1)}, u32[]{:S(2)}) copy-start(bf16[256,1024]{1,0:T(8,128)(2,1)S(1)} %shard_map.119.refs_0_.refs_13_) | copy-start | bytes 1572868
  116.0 3.4 %collective-permute-start.16 = (bf16[256,1024]{1,0:T(8,128)(2,1)S(1)}, bf16[256,1024]{1,0:T(8,128)(2,1)S(1)}, u32[]{:S(2)}, u32[]{:S(2)}) collective-permute-start(bf16[256,1024]{1,0:T(8,128)(2,1)S(1)} %shard_map.119.refs_0_.refs_13_), channel_id=1, source_target_pairs={{0,4},{4,0},{8,12},{12,8},{16,20},{20,16},{24,28},{28,24},{32,36},... | collective-permute-start | bytes 1572872 | tf_op jit(solution)/shard_map/ppermute | solution.py:264
  119.4 1.9 collective-permute-start.17
  123.0 6.5 %copy-start.4 = (bf16[1024,384]{1,0:T(8,128)(2,1)}, bf16[1024,384]{1,0:T(8,128)(2,1)S(1)}, u32[]{:S(2)}) copy-start(bf16[1024,384]{1,0:T(8,128)(2,1)S(1)} %get-tuple-element.39.refs_0_.refs_21_) | copy-start | bytes 2359300
  124.9 3.9 %collective-permute-start.18 = (bf16[512,1024]{1,0:T(8,128)(2,1)S(1)}, bf16[512,1024]{1,0:T(8,128)(2,1)S(1)}, u32[]{:S(2)}, u32[]{:S(2)}) collective-permute-start(bf16[512,1024]{1,0:T(8,128)(2,1)S(1)} %get-tuple-element.41), channel_id=1, source_target_pairs={{0,4},{4,0},{8,12},{12,8},{16,20},{20,16},{24,28},{28,24},{32,36},... | collective-permute-start | bytes 3145736 | tf_op jit(solution)/shard_map/ppermute | solution.py:264
  128.0 6.9 %collective-permute-start.20 = (bf16[512,1024]{1,0:T(8,128)(2,1)S(1)}, bf16[512,1024]{1,0:T(8,128)(2,1)S(1)}, u32[]{:S(2)}, u32[]{:S(2)}) collective-permute-start(bf16[512,1024]{1,0:T(8,128)(2,1)S(1)} %get-tuple-element.46), channel_id=1, source_target_pairs={{0,4},{4,0},{8,12},{12,8},{16,20},{20,16},{24,28},{28,24},{32,36},... | collective-permute-start | bytes 3145736 | tf_op jit(solution)/shard_map/ppermute | solution.py:264
  128.4 6.4 %collective-permute-start.22 = (bf16[512,1024]{1,0:T(8,128)(2,1)S(1)}, bf16[512,1024]{1,0:T(8,128)(2,1)S(1)}, u32[]{:S(2)}, u32[]{:S(2)}) collective-permute-start(bf16[512,1024]{1,0:T(8,128)(2,1)S(1)} %get-tuple-element.48), channel_id=1, source_target_pairs={{0,4},{4,0},{8,12},{12,8},{16,20},{20,16},{24,28},{28,24},{32,36},... | collective-permute-start | bytes 3145736 | tf_op jit(solution)/shard_map/ppermute | solution.py:264
  131.3 31.0 %collective-permute-start.19 = (bf16[512,1024]{1,0:T(8,128)(2,1)S(1)}, bf16[512,1024]{1,0:T(8,128)(2,1)S(1)}, u32[]{:S(2)}, u32[]{:S(2)}) collective-permute-start(bf16[512,1024]{1,0:T(8,128)(2,1)S(1)} %get-tuple-element.45), channel_id=1, source_target_pairs={{0,4},{4,0},{8,12},{12,8},{16,20},{20,16},{24,28},{28,24},{32,36},... | collective-permute-start | bytes 3145736 | tf_op jit(solution)/shard_map/ppermute | solution.py:264
  131.6 15.4 %collective-permute-start.23 = (bf16[256,1024]{1,0:T(8,128)(2,1)S(1)}, bf16[256,1024]{1,0:T(8,128)(2,1)S(1)}, u32[]{:S(2)}, u32[]{:S(2)}) collective-permute-start(bf16[256,1024]{1,0:T(8,128)(2,1)S(1)} %get-tuple-element.49), channel_id=1, source_target_pairs={{0,3},{1,0},{2,1},{3,2},{4,7},{5,4},{6,5},{7,6},{8,11},{9,8},{10,9... | collective-permute-start | bytes 1572872 | tf_op jit(solution)/shard_map/ppermute | solution.py:261
  131.6 15.4 %collective-permute-start.21 = (bf16[256,1024]{1,0:T(8,128)(2,1)S(1)}, bf16[256,1024]{1,0:T(8,128)(2,1)S(1)}, u32[]{:S(2)}, u32[]{:S(2)}) collective-permute-start(bf16[256,1024]{1,0:T(8,128)(2,1)S(1)} %get-tuple-element.43.refs_3_), channel_id=1, source_target_pairs={{0,1},{1,2},{2,3},{3,0},{4,5},{5,6},{6,7},{7,4},{8,9},{9,10},{10,1... | collective-permute-start | bytes 1572872 | tf_op jit(solution)/shard_map/ppermute | solution.py:258
  149.0 9.7 %collective-permute-start.24 = (bf16[512,256]{1,0:T(8,128)(2,1)S(1)}, bf16[512,256]{1,0:T(8,128)(2,1)S(1)}, u32[]{:S(2)}, u32[]{:S(2)}) collective-permute-start(bf16[512,256]{1,0:T(8,128)(2,1)S(1)} %get-tuple-element.50), channel_id=1, source_target_pairs={{0,1},{1,2},{2,3},{3,0},{4,5},{5,6},{6,7},{7,4},{8,9},{9,10},{10,1... | collective-permute-start | bytes 786440 | tf_op jit(solution)/shard_map/ppermute | solution.py:258
  151.9 10.5 %collective-permute-start.25 = (bf16[512,256]{1,0:T(8,128)(2,1)S(1)}, bf16[512,256]{1,0:T(8,128)(2,1)S(1)}, u32[]{:S(2)}, u32[]{:S(2)}) collective-permute-start(bf16[512,256]{1,0:T(8,128)(2,1)S(1)} %get-tuple-element.51), channel_id=1, source_target_pairs={{0,3},{1,0},{2,1},{3,2},{4,7},{5,4},{6,5},{7,6},{8,11},{9,8},{10,9... | collective-permute-start | bytes 786440 | tf_op jit(solution)/shard_map/ppermute | solution.py:261
  151.9 25.8 %collective-permute-start.26 = (bf16[512,768]{1,0:T(8,128)(2,1)}, bf16[512,768]{1,0:T(8,128)(2,1)}, u32[]{:S(2)}, u32[]{:S(2)}) collective-permute-start(bf16[512,768]{1,0:T(8,128)(2,1)} %get-tuple-element.52), channel_id=1, source_target_pairs={{0,1},{1,2},{2,3},{3,0},{4,5},{5,6},{6,7},{7,4},{8,9},{9,10},{10,1... | collective-permute-start | bytes 2359304 | tf_op jit(solution)/shard_map/ppermute | solution.py:258
  155.2 22.5 %collective-permute-start.27 = (bf16[512,768]{1,0:T(8,128)(2,1)}, bf16[512,768]{1,0:T(8,128)(2,1)}, u32[]{:S(2)}, u32[]{:S(2)}) collective-permute-start(bf16[512,768]{1,0:T(8,128)(2,1)} %get-tuple-element.53), channel_id=1, source_target_pairs={{0,3},{1,0},{2,1},{3,2},{4,7},{5,4},{6,5},{7,6},{8,11},{9,8},{10,9... | collective-permute-start | bytes 2359304 | tf_op jit(solution)/shard_map/ppermute | solution.py:261
  163.8 23.1 %all-to-all-start.2 = ((bf16[32,16,256]{2,1,0:T(8,128)(2,1)}), bf16[32,16,256]{2,1,0:T(8,128)(2,1)}, u32[]{:S(2)}, u32[]{:S(2)}) async-start(bf16[32,16,256]{2,1,0:T(8,128)(2,1)} %bitcast.9), calls=%async_computation.2 | async-start | bytes 524288 | tf_op jit(solution)/shard_map/all_to_all | solution.py:269
  186.9 26.5 %all-to-all-start.3 = ((bf16[32,16,768]{2,1,0:T(8,128)(2,1)}), bf16[32,16,768]{2,1,0:T(8,128)(2,1)}, u32[]{:S(2)}, u32[]{:S(2)}) async-start(bf16[32,16,768]{2,1,0:T(8,128)(2,1)} %bitcast.11), calls=%async_computation.3 | async-start | bytes 1572864 | tf_op jit(solution)/shard_map/all_to_all | solution.py:269
  (7 other events, 18.1 us)
